TPU v7x, 128 devices: a whole 4x4x4 slice. The times are simulated.
128 devices in a mesh: dp: 32 (over y_lo, x, z), mp: 4 (over y_hi, core).
Axes of the slice: x: 4, y: 4 (y_hi: 2, y_lo: 2; y = y_hi * 2 + y_lo), z: 4, core: 2. Of those that a mesh axis runs over, the one named last changes fastest.
Arguments:
- stream: bfloat16 [32, 512, 2048], P('dp'), may hold values from -6 to 6
- code_ids: int32 [32, 512], P('dp'), may hold values from 0 to 4095
- segment_ids: int32 [32, 512], P('dp'), may hold values from 0 to 3, never falling along the last dimension, each value on 1 to 256 neighbouring positions
- padding: int32 [32, 512], P('dp'), may hold values from 0 to 1, as said below
- codebook: bfloat16 [4096, 2048], replicated, may hold values from -6 to 6
- norm1_gain: bfloat16 [2048], P('dp'), may hold values from 0.099609375 to 1.8984375
- norm1_shift: bfloat16 [2048], P('dp'), may hold values from -3 to 3
- w_qkv: bfloat16 [2048, 3, 2048], P('dp', None, 'mp'), may hold values from -0.125 to 0.125
- w_out: bfloat16 [2048, 2048], P('dp', 'mp'), may hold values from -0.75 to 0.75
- norm2_gain: bfloat16 [2048], P('dp'), may hold values from 0.099609375 to 1.8984375
- norm2_shift: bfloat16 [2048], P('dp'), may hold values from -3 to 3
- w_up: bfloat16 [2048, 8192], P('dp', 'mp'), may hold values from -0.125 to 0.125
- w_down: bfloat16 [2048, 8192], P('dp', 'mp'), may hold values from -0.0625 to 0.0625
- cotangent: bfloat16 [32, 512, 2048], P('dp'), may hold values from -6 to 6
Outputs:
- layer_out: float32 [32, 512, 2048], P('dp')
- input_grad: float32 [32, 512, 2048], P('dp')
- grad_norm1_gain: float32 [2048], P('dp')
- grad_norm1_shift: float32 [2048], P('dp')
- grad_w_qkv: float32 [2048, 3, 2048], P('dp', None, 'mp')
- grad_w_out: float32 [2048, 2048], P('dp', 'mp')
- grad_norm2_gain: float32 [2048], P('dp')
- grad_norm2_shift: float32 [2048], P('dp')
- grad_w_up: float32 [2048, 8192], P('dp', 'mp')
- grad_w_down: float32 [2048, 8192], P('dp', 'mp')
Inputs may be any that keep to these rules, and one draw needn't show every extreme that they name: In each row the real tokens come first and the last 1 to 128 positions are padding. `segment_ids`: episode numbers never fall along a row; an episode spans at most 256 positions.
All inputs are finite; a program needn't handle non-finite values.
Results may differ from a plain program's by a relative error of at most 0.028.
Values may be sent and summed in bfloat16 or wider, within the bound.
A program may use at most 192 MiB of HBM per device.

v0:
```python
import functools

import jax
import jax.numpy as jnp
from jax import lax
from jax.experimental import pallas as pl
from jax.experimental.pallas import tpu as pltpu
from jax.sharding import PartitionSpec as P

HEAD = 128
WIDTH = 2048
SHARE = 128
PART = 1024
MESH = pl.DeviceIdType.MESH
ANY = pl.BlockSpec(memory_space=pl.ANY)
VMEM = pl.BlockSpec(memory_space=pltpu.VMEM)
masked_score = -1000000000.0
epsilon = 1e-05
f32 = jnp.float32
bf16 = jnp.bfloat16


def place():
    dp, mp = lax.axis_index("dp"), lax.axis_index("mp")
    return lax.div(dp, 16), lax.rem(lax.div(dp, 4), 4), lax.rem(dp, 4), lax.div(mp, 2), lax.rem(mp, 2)


def ring(position, step):
    return lax.rem(position + step + 4, 4)


def xz_neighbour(axis, step):
    ylo, x, z, yhi, core = place()
    if axis == 0:
        x = ring(x, step)
    else:
        z = ring(z, step)
    return (ylo * 16 + x * 4 + z, yhi * 2 + core)


def y_peer(step):
    ylo, x, z, yhi, core = place()
    y = ring(yhi * 2 + ylo, step)
    return (lax.rem(y, 2) * 16 + x * 4 + z, lax.div(y, 2) * 2 + core)


def lo_partner():
    ylo, x, z, yhi, core = place()
    return ((1 - ylo) * 16 + x * 4 + z, yhi * 2 + core)


def core_partner():
    ylo, x, z, yhi, core = place()
    return (ylo * 16 + x * 4 + z, yhi * 2 + 1 - core)


def greet(peers):
    barrier = pltpu.get_barrier_semaphore()
    for peer in peers:
        pl.semaphore_signal(barrier, inc=1, device_id=peer, device_id_type=MESH)
    pl.semaphore_wait(barrier, len(peers))


def remote(src, dst, send_sem, recv_sem, peer):
    return pltpu.make_async_remote_copy(
        src_ref=src,
        dst_ref=dst,
        send_sem=send_sem,
        recv_sem=recv_sem,
        device_id=peer,
        device_id_type=MESH,
    )


def sems(*shape):
    return pltpu.SemaphoreType.DMA(shape)


def params(collective_id, mib=48):
    return pltpu.CompilerParams(
        collective_id=collective_id, has_side_effects=True, vmem_limit_bytes=mib << 20
    )


PEERS = {
    "core": core_partner,
    "x+": lambda: xz_neighbour(0, 1),
    "x-": lambda: xz_neighbour(0, -1),
    "z+": lambda: xz_neighbour(1, 1),
    "z-": lambda: xz_neighbour(1, -1),
    "y1": lambda: y_peer(1),
    "y2": lambda: y_peer(2),
    "y3": lambda: y_peer(3),
}


def dp_peer(step):
    return (lax.rem(lax.axis_index("dp") + step, 32), lax.axis_index("mp"))


def diagonal_peer(step):
    dp, mp = y_peer(step)
    return (dp, mp + 1 - 2 * lax.rem(mp, 2))


def mp_peer(step):
    return (lax.axis_index("dp"), lax.rem(lax.axis_index("mp") + step, 4))


PEERS.update({f"dp{k}": functools.partial(dp_peer, k) for k in range(1, 32)})
PEERS.update({f"mp{k}": functools.partial(mp_peer, k) for k in range(1, 4)})
PEERS.update({f"d{k}": functools.partial(diagonal_peer, k) for k in range(1, 4)})
GROUP = ["y1", "y2", "y3", "core", "d1", "d2", "d3"]
DP = [f"dp{k}" for k in range(1, 32)]
MP = ["mp1", "mp2", "mp3"]


def kernel_call(body, jobs, peers, ins, outs, scratch, collective_id, mib=56):
    def kernel(*refs):
        taken = 0

        def take(count):
            nonlocal taken
            taken += count
            return refs[taken - count : taken]

        groups = [take(len(ins)), take(len(outs)), take(len(scratch))]
        makers = []
        for job in jobs:
            own = take(len(job["scratch"]))
            makers.append(lambda *given, job=job, own=own: job["steps"](*given, *own))
        greet([PEERS[name]() for name in peers])
        body(*groups, makers)

    return pl.pallas_call(
        kernel,
        out_shape=[shape for shape, _ in outs],
        in_specs=[spec for _, spec in ins],
        out_specs=[spec for _, spec in outs],
        scratch_shapes=scratch + [one for job in jobs for one in job["scratch"]],
        compiler_params=params(collective_id, mib),
    )(*[array for array, _ in ins])


def finish(*runs):
    for run in runs:
        for _ in run:
            pass


def step(*runs):
    for run in runs:
        next(run, None)


def shaped(dtype, *shape):
    return jax.ShapeDtypeStruct(shape, dtype)


def small_gather():
    def steps(own, everyone, send, recv):
        dp, mp = lax.axis_index("dp"), lax.axis_index("mp")

        def move(k):
            return remote(own, everyone.at[dp], send.at[k], recv.at[dp], dp_peer(k))

        def start(k, carry):
            move(k).start()
            return carry

        lax.fori_loop(1, 32, start, 0)
        everyone[dp] = own[...]
        yield

        def end(k, carry):
            source = lax.rem(dp + k, 32)
            move(k).wait_send()
            remote(own, everyone.at[source], send.at[k], recv.at[source], dp_peer(k)).wait_recv()
            return carry

        lax.fori_loop(1, 32, end, 0)

    return {"scratch": [sems(32), sems(32)], "steps": steps}


def small_reduce():
    def steps(rows, out, arrived, summed, more, send, recv, send_two, recv_two):
        dp = lax.axis_index("dp")

        def move(k):
            tile = lax.div(lax.rem(dp + k, 32), 2)
            src = rows.at[:, pl.ds(pl.multiple_of(tile * 128, 128), 128)]
            return remote(src, arrived.at[k], send.at[k], recv.at[k], dp_peer(k))

        def start(k, carry):
            move(k).start()
            return carry

        def add(k, total):
            move(k).wait()
            return total + arrived[k]

        lax.fori_loop(1, 32, start, 0)
        yield
        mine = rows[:, pl.ds(pl.multiple_of(lax.div(dp, 2) * 128, 128), 128)]
        summed[...] = lax.fori_loop(1, 32, add, mine)
        copies = [
            remote(summed, more.at[k - 1], send_two.at[k], recv_two.at[k], mp_peer(k))
            for k in (1, 2, 3)
        ]
        for copy in copies:
            copy.start()
        yield
        for copy in copies:
            copy.wait()
        out[...] = summed[...] + more[0] + more[1] + more[2]

    return {
        "scratch": [
            pltpu.VMEM((32, 8, 128), f32),
            pltpu.VMEM((8, 128), f32),
            pltpu.VMEM((3, 8, 128), f32),
            sems(32),
            sems(32),
            sems(4),
            sems(4),
        ],
        "steps": steps,
    }


def row_exchange(count=1):
    def steps(halves, full, local_sem, send, recv):
        ylo, x, z, yhi, core = place()
        up, down, other = y_peer(1), y_peer(3), core_partner()
        first = []
        for n in range(count):
            for u, peer in ((0, up), (1, down)):
                here = full.at[n, ylo, core, u]
                first.append(remote(halves.at[n, u], here, send.at[n, u], recv.at[n, u], peer))
        for n in range(count):
            here = full.at[n, ylo, core]
            first.append(remote(halves.at[n], here, send.at[n, 2], recv.at[n, 2], other))
        for copy in first:
            copy.start()
        local = [
            pltpu.make_async_copy(halves.at[n], full.at[n, ylo, core], local_sem.at[n])
            for n in range(count)
        ]
        for copy in local:
            copy.start()
        yield
        second = []
        for n in range(count):
            for u in range(2):
                here = full.at[n, 1 - ylo, core, u]
                remote(halves.at[n, u], here, send.at[n, u], recv.at[n, u], up).wait_recv()
                copy = remote(here, here, send.at[n, 3 + u], recv.at[n, 3 + u], other)
                copy.start()
                second.append(copy)
        yield
        for n in range(count):
            here = full.at[n, ylo, 1 - core]
            remote(halves.at[n], here, send.at[n, 2], recv.at[n, 2], other).wait_recv()
            for u in range(2):
                here = full.at[n, 1 - ylo, 1 - core, u]
                remote(here, here, send.at[n, 3 + u], recv.at[n, 3 + u], other).wait_recv()
        for copy in first + second:
            copy.wait_send()
        for copy in local:
            copy.wait()

    return {
        "scratch": [sems(count), sems(count, 5), sems(count, 5)],
        "steps": steps,
    }


def share_gather():
    def steps(share, full, local_sem, send, recv):
        ylo, x, z, yhi, core = place()
        y = yhi * 2 + ylo
        other = core_partner()
        half = SHARE // 2
        sent = []

        def of(step, half_core):
            source = ring(y, step)
            return full.at[lax.rem(source, 2), half_core, lax.div(source, 2)]

        def go(src, dst, n, peer):
            copy = remote(src, dst, send.at[n], recv.at[n], peer)
            copy.start()
            sent.append(copy)

        def came(dst, n):
            remote(dst, dst, send.at[n], recv.at[n], other).wait_recv()

        local = pltpu.make_async_copy(share, of(0, core), local_sem)
        go(share, of(0, core), 0, y_peer(1))
        go(share, of(0, core), 1, y_peer(3))
        go(share, of(0, core), 2, other)
        local.start()
        yield
        for n, step_back, rows, onward in ((0, 3, pl.ds(0, half), 1), (1, 1, pl.ds(half, half), 3)):
            here = of(step_back, core)
            came(here, n)
            go(here.at[rows], here.at[rows], 3 + n, y_peer(onward))
            go(here, here, 5 + n, other)
        yield
        far = of(2, core)
        came(far.at[pl.ds(0, half)], 3)
        came(far.at[pl.ds(half, half)], 4)
        go(far, far, 7, other)
        yield
        came(of(0, 1 - core), 2)
        came(of(3, 1 - core), 5)
        came(of(1, 1 - core), 6)
        came(of(2, 1 - core), 7)
        for copy in sent:
            copy.wait_send()
        local.wait()

    return {"scratch": [pltpu.SemaphoreType.DMA, sems(8), sems(8)], "steps": steps}


def add_rows(count, one):
    def body(i, carry):
        one(pl.ds(pl.multiple_of(i * 16, 16), 16))
        return carry

    lax.fori_loop(0, count // 16, body, 0)


def share_sum():
    def steps(partial, out, from_core, via, arrived, send, recv, send_two, recv_two):
        ylo, x, z, yhi, core = place()
        y = yhi * 2 + ylo
        other = core_partner()
        half = SHARE // 2

        def block(k, half_core):
            target = ring(y, k)
            return partial.at[lax.rem(target, 2), half_core, lax.div(target, 2)]

        first, second = {}, {}

        def to_core(order):
            for k in order:
                first[k] = remote(block(k, 1 - core), from_core.at[k], send.at[k], recv.at[k], other)
                first[k].start()

        to_core((2, 0))
        yield
        first[2].wait_recv()
        far = block(2, core)

        def add_far(rows):
            far[rows] = (far[rows].astype(f32) + from_core[2, rows].astype(f32)).astype(bf16)

        add_rows(SHARE, add_far)
        for n, k in ((0, 1), (1, 3)):
            second[n] = remote(
                far.at[pl.ds(half * n, half)], via.at[n], send_two.at[n], recv_two.at[n], y_peer(k)
            )
            second[n].start()
        yield
        to_core((1, 3))
        yield
        for n, k in ((0, 1), (1, 3)):
            first[k].wait_recv()
            second[n].wait_recv()
            near = block(k, core)

            def add_via(i, carry):
                at = pl.multiple_of(i * 16, 16)
                rows, with_via = pl.ds(at, 16), pl.ds(pl.multiple_of(half * n + at, 16), 16)
                value = near[with_via].astype(f32) + from_core[k, with_via].astype(f32)
                near[with_via] = (value + via[n, rows].astype(f32)).astype(bf16)
                plain = pl.ds(pl.multiple_of(half * (1 - n) + at, 16), 16)
                value = near[plain].astype(f32) + from_core[k, plain].astype(f32)
                near[plain] = value.astype(bf16)
                return carry

            lax.fori_loop(0, half // 16, add_via, 0)
            second[2 + n] = remote(near, arrived.at[n], send_two.at[2 + n], recv_two.at[2 + n], y_peer(k))
            second[2 + n].start()
        yield
        first[0].wait_recv()
        second[2].wait_recv()
        second[3].wait_recv()
        mine_own = block(0, core)

        def total(rows):
            value = mine_own[rows].astype(f32) + from_core[0, rows].astype(f32)
            out[rows] = value + arrived[0, rows].astype(f32) + arrived[1, rows].astype(f32)

        add_rows(SHARE, total)
        for k in range(4):
            first[k].wait_send()
            second[k].wait_send()

    return {
        "scratch": [
            pltpu.VMEM((4, SHARE, WIDTH), bf16),
            pltpu.VMEM((2, SHARE // 2, WIDTH), bf16),
            pltpu.VMEM((2, SHARE, WIDTH), bf16),
        ]
        + [sems(4)] * 4,
        "steps": steps,
    }


def feature_start(ylo, yhi, core):
    return pl.multiple_of((yhi * 2 + core) * 512 + ylo * 256, 256)


def heads_to_tokens():
    def steps(heads, tokens, send, recv):
        ylo, x, z, yhi, core = place()
        y = yhi * 2 + ylo
        mine = tokens.at[:, pl.ds(feature_start(ylo, yhi, core), 256)]
        sent = []

        def go(k, flip):
            target = ring(y, k)
            half = 1 - core if flip else core
            peer = diagonal_peer(k) if flip else y_peer(k)
            src = heads.at[lax.rem(target, 2), half, lax.div(target, 2)]
            copy = remote(src, mine, send.at[2 * k + flip], recv.at[2 * k + flip], peer)
            copy.start()
            sent.append(copy)

        for k in (1, 3):
            for flip in (0, 1):
                go(k, flip)
        yield
        for k, flip in ((2, 0), (2, 1), (0, 1)):
            go(k, flip)
        tokens[:, pl.ds(feature_start(ylo, yhi, core), 256)] = heads[ylo, core, yhi]
        yield
        for k, flip in ((1, 0), (1, 1), (3, 0), (3, 1), (2, 0), (2, 1), (0, 1)):
            source = ring(y, -k)
            half = 1 - core if flip else core
            start = feature_start(lax.rem(source, 2), lax.div(source, 2), half)
            here = tokens.at[:, pl.ds(start, 256)]
            remote(heads.at[0, 0, 0], here, send.at[2 * k + flip], recv.at[2 * k + flip], y_peer(1)).wait_recv()
        for copy in sent:
            copy.wait_send()

    return {"scratch": [sems(8), sems(8)], "steps": steps}


def tokens_to_heads():
    def steps(tokens, heads, send, recv):
        ylo, x, z, yhi, core = place()
        y = yhi * 2 + ylo
        mine = heads.at[ylo, core, yhi]
        sent = []
        order = ((1, 0), (1, 1), (3, 0), (3, 1), (2, 0), (2, 1), (0, 1))
        for k, flip in order:
            target = ring(y, k)
            half = 1 - core if flip else core
            peer = diagonal_peer(k) if flip else y_peer(k)
            start = feature_start(lax.rem(target, 2), lax.div(target, 2), half)
            src = tokens.at[:, pl.ds(start, 256)]
            copy = remote(src, mine, send.at[2 * k + flip], recv.at[2 * k + flip], peer)
            copy.start()
            sent.append(copy)
        heads[ylo, core, yhi] = tokens[:, pl.ds(feature_start(ylo, yhi, core), 256)]
        yield
        for k, flip in order:
            source = ring(y, -k)
            half = 1 - core if flip else core
            here = heads.at[lax.rem(source, 2), half, lax.div(source, 2)]
            remote(here, here, send.at[2 * k + flip], recv.at[2 * k + flip], y_peer(1)).wait_recv()
        for copy in sent:
            copy.wait_send()

    return {"scratch": [sems(8), sems(8)], "steps": steps}


def row_gather():
    def steps(share, full, local_sem, send, recv):
        ylo, x, z, yhi, core = place()
        across, other = y_peer(2), core_partner()
        mine = full.at[:, core, yhi]
        far = full.at[:, core, 1 - yhi]
        local = pltpu.make_async_copy(share, mine, local_sem)
        one = remote(share, mine, send.at[0], recv.at[0], across)
        two = remote(share, mine, send.at[1], recv.at[1], other)
        one.start()
        two.start()
        local.start()
        yield
        remote(share, far, send.at[0], recv.at[0], across).wait_recv()
        three = remote(far, far, send.at[2], recv.at[2], other)
        three.start()
        yield
        remote(share, full.at[:, 1 - core, yhi], send.at[1], recv.at[1], other).wait_recv()
        last = full.at[:, 1 - core, 1 - yhi]
        remote(last, last, send.at[2], recv.at[2], other).wait_recv()
        for copy in (one, two, three):
            copy.wait_send()
        local.wait()

    return {
        "scratch": [pltpu.SemaphoreType.DMA, sems(3), sems(3)],
        "steps": steps,
    }


SIGNS = (1, -1)
XZ = ["x+", "x-", "z+", "z-"]


def xz_near():
    return [[xz_neighbour(axis, d) for d in SIGNS] for axis in (0, 1)]


def weight_gather(columns, spread=False, flat=False):
    count = 4 if spread else 2

    def steps(own, full, local_sem, swap_send, swap_recv, send, recv):
        ylo, x, z, yhi, core = place()
        y = yhi * 2 + ylo
        near = xz_near()
        offsets = (0, -1, 1, 2)

        def move(src, dst, s, r, stage, d, axis):
            n = ((s * 2 + r) * 8 + stage) * 2 + d
            return remote(src, dst, send.at[n], recv.at[n], near[axis][d])

        def origin(s):
            if spread:
                return ring(y, offsets[s])
            return ylo if s == 0 else 1 - ylo

        def block(s, r, one, two, rows):
            if r == 0:
                return full.at[origin(s), ring(x, one), ring(z, two), rows]
            return full.at[origin(s), ring(x, two), ring(z, one), rows]

        def rows_of(r, d=None):
            return pl.ds(32 * r, 32) if d is None else pl.ds(32 * r + 16 * d, 16)

        def half(n):
            if flat:
                return own.at[:, pl.ds(pl.multiple_of(n * columns, columns), columns)]
            return own.at[n]

        mine = own if spread else half(ylo)
        here = full.at[origin(0), x, z]
        local = pltpu.make_async_copy(mine, here, local_sem)
        swaps = []
        for s in range(1, count):
            peer = y_peer((4 - offsets[s]) % 4) if spread else lo_partner()
            src = own if spread else half(1 - ylo)
            swaps.append(remote(src, here, swap_send.at[s], swap_recv.at[s], peer))
        for swap in swaps:
            swap.start()
        sent = []

        def go(*args):
            copy = move(*args)
            copy.start()
            sent.append(copy)

        def begin(s, source):
            for r in range(2):
                for d in range(2):
                    src = source.at[rows_of(r)]
                    go(src, block(s, r, 0, 0, rows_of(r)), s, r, 0, d, r)
            for r in range(2):
                for d in range(2):
                    src = source.at[rows_of(r)]
                    go(src, block(s, r, 0, 0, rows_of(r)), s, r, 2, d, 1 - r)

        begin(0, mine)
        local.start()
        yield
        for s in range(1, count):
            came = full.at[origin(s), x, z]
            remote(came, came, swap_send.at[s], swap_recv.at[s], lo_partner()).wait_recv()
            begin(s, came)
        yield
        for s in range(count):
            for r in range(2):
                for d in range(2):
                    came = block(s, r, -SIGNS[d], 0, rows_of(r))
                    move(came, came, s, r, 0, d, r).wait_recv()
                    piece = block(s, r, -SIGNS[d], 0, rows_of(r, d))
                    go(piece, piece, s, r, 1, d, r)
                for part in (1, 2):
                    for d in range(2):
                        came = block(s, r, offsets[part], 0, rows_of(r))
                        go(came, came, s, r, 2 + part, d, 1 - r)
            if s % 2:
                yield
        for s in range(count):
            for r in range(2):
                for d in range(2):
                    piece = block(s, r, 2, 0, rows_of(r, d))
                    move(piece, piece, s, r, 1, d, r).wait_recv()
                for d in range(2):
                    came = block(s, r, 2, 0, rows_of(r))
                    go(came, came, s, r, 5, d, 1 - r)
            if s % 2:
                yield
        for part in (0, 2, 1, 3):
            d = part // 2
            for s in range(count):
                for r in range(2):
                    came = block(s, r, offsets[part], -SIGNS[d], rows_of(r))
                    move(came, came, s, r, 2 + part, d, 1 - r).wait_recv()
                    go(came, came, s, r, 6 + part % 2, d, 1 - r)
            yield
        for s in range(count):
            for r in range(2):
                for part in range(4):
                    d = 1 - part // 2
                    came = block(s, r, offsets[part], -SIGNS[d], rows_of(r))
                    move(came, came, s, r, 2 + part, d, 1 - r).wait_recv()
                for part in range(4):
                    d = part // 2
                    came = block(s, r, offsets[part], 2, rows_of(r))
                    move(came, came, s, r, 6 + part % 2, d, 1 - r).wait_recv()
        for copy in sent + swaps:
            copy.wait_send()
        local.wait()

    return {
        "scratch": [pltpu.SemaphoreType.DMA, sems(count), sems(count), sems(32 * count), sems(32 * count)],
        "steps": steps,
    }


def gathered(columns, count=2):
    return (shaped(bf16, count, 4, 4, 64, columns), ANY)


def weight_sum(columns=PART):
    def steps(grads, out, wide, thin, total, swap_send, swap_recv, send, recv):
        ylo, x, z, yhi, core = place()
        near = xz_near()
        partner = lo_partner()

        def move(src, dst, s, r, stage, d, axis):
            n = ((s * 2 + r) * 6 + stage) * 2 + d
            return remote(src, dst, send.at[n], recv.at[n], near[axis][d])

        def line(s, r, step, part):
            if r == 0:
                return grads.at[s, part, ring(z, step), pl.ds(0, 32)]
            return grads.at[s, ring(x, step), part, pl.ds(32, 32)]

        def block(s, r, step, rows):
            if r == 0:
                return grads.at[s, ring(x, step), z, rows]
            return grads.at[s, x, ring(z, step), rows]

        def wide_move(s, r, d, kind):
            if kind == 0:
                src = line(s, r, 2, pl.ds(2 * d, 2))
            elif kind == 1:
                src = line(s, r, SIGNS[d], pl.ds(2 - 2 * d, 2))
            else:
                src = line(s, r, SIGNS[d], pl.ds(2 * d, 2))
            return move(src, wide.at[s, r, kind, d], s, r, kind, d, 1 - r)

        def thin_move(s, r, d, kind):
            if kind == 0:
                src = block(s, r, 2, pl.ds(32 * r + 16 * d, 16))
            elif kind == 1:
                src = block(s, r, SIGNS[d], pl.ds(32 * r + 16 - 16 * d, 16))
            else:
                src = block(s, r, SIGNS[d], pl.ds(32 * r + 16 * d, 16))
            return move(src, thin.at[s, r, kind, d], s, r, 3 + kind, d, r)

        for s in range(2):
            for kind in range(2):
                for r in range(2):
                    for d in range(2):
                        wide_move(s, r, d, kind).start()
        yield

        for s in range(2):
            for r in range(2):
                for d in range(2):
                    wide_move(s, r, d, 0).wait_recv()
                    for p in range(2):
                        mine = line(s, r, SIGNS[d], 2 * d + p)

                        def one(rows):
                            value = mine[rows].astype(f32) + wide[s, r, 0, d, p, rows].astype(f32)
                            mine[rows] = value.astype(bf16)

                        add_rows(32, one)
                    wide_move(s, r, d, 2).start()
            yield

        for s in range(2):
            for r in range(2):
                for d in range(2):
                    wide_move(s, r, d, 1).wait_recv()
                    wide_move(s, r, d, 2).wait_recv()
                for p in range(4):
                    mine = line(s, r, 0, p)
                    d = p // 2

                    def one(rows):
                        value = mine[rows].astype(f32) + wide[s, r, 2, d, p % 2, rows].astype(f32)
                        value += wide[s, r, 1, 1 - d, p % 2, rows].astype(f32)
                        mine[rows] = value.astype(bf16)

                    add_rows(32, one)
                for kind in range(2):
                    for d in range(2):
                        thin_move(s, r, d, kind).start()
            yield

        for s in range(2):
            for r in range(2):
                for d in range(2):
                    thin_move(s, r, d, 0).wait_recv()
                    mine = block(s, r, SIGNS[d], pl.ds(32 * r + 16 * d, 16))
                    value = mine[...].astype(f32) + thin[s, r, 0, d].astype(f32)
                    mine[...] = value.astype(bf16)
                    thin_move(s, r, d, 2).start()
        yield

        for s in range(2):
            for r in range(2):
                for d in range(2):
                    thin_move(s, r, d, 1).wait_recv()
                    thin_move(s, r, d, 2).wait_recv()
                for d in range(2):
                    rows = pl.ds(32 * r + 16 * d, 16)
                    value = block(s, r, 0, rows)[...].astype(f32) + thin[s, r, 2, d].astype(f32)
                    value += thin[s, r, 1, 1 - d].astype(f32)
                    total[s, rows] = value.astype(bf16)
        swap = remote(total.at[1 - ylo], out.at[ylo], swap_send, swap_recv, partner)
        swap.start()
        out[ylo] = total[ylo]
        yield
        for s in range(2):
            for r in range(2):
                for d in range(2):
                    for kind in range(3):
                        wide_move(s, r, d, kind).wait_send()
                        thin_move(s, r, d, kind).wait_send()
        remote(total.at[0], out.at[1 - ylo], swap_send, swap_recv, partner).wait_recv()
        swap.wait_send()

    return {
        "scratch": [
            pltpu.VMEM((2, 2, 3, 2, 2, 32, columns), bf16),
            pltpu.VMEM((2, 2, 3, 2, 16, columns), bf16),
            pltpu.VMEM((2, 64, columns), bf16),
            pltpu.SemaphoreType.DMA,
            pltpu.SemaphoreType.DMA,
            sems(48),
            sems(48),
        ],
        "steps": steps,
    }


def standardize(value):
    mean = jnp.mean(value, axis=-1, keepdims=True)
    centered = value - mean
    scale_inv = lax.rsqrt(jnp.mean(centered * centered, axis=-1, keepdims=True) + epsilon)
    return (centered * scale_inv, scale_inv)


def norm_back(grad_normed_out, normed, scale_inv, gain):
    scaled = grad_normed_out * gain
    mean_one = jnp.mean(scaled, axis=-1, keepdims=True)
    mean_two = jnp.mean(scaled * normed, axis=-1, keepdims=True)
    grad_value = scale_inv * (scaled - mean_one - normed * mean_two)
    grad_gain = jnp.sum(grad_normed_out * normed, axis=0, keepdims=True)
    grad_shift = jnp.sum(grad_normed_out, axis=0, keepdims=True)
    return (grad_value, grad_gain, grad_shift)


def dot(a, b):
    return jnp.dot(a, b, preferred_element_type=f32)


def turned_dot(a, b):
    return lax.dot_general(a, b, (((1,), (1,)), ((), ())), preferred_element_type=f32)


def outer_dot(a, b):
    return lax.dot_general(a, b, (((0,), (0,)), ((), ())), preferred_element_type=f32)


def some_rows(count, size, one):
    def body(i, carry):
        one(pl.ds(pl.multiple_of(i * size, size), size))
        return carry

    lax.fori_loop(0, count // size, body, 0)


def fetched(src, dst, sem):
    copy = pltpu.make_async_copy(src, dst, sem)
    copy.start()
    return copy


CODES = 4096
CODE_CHUNK = 1024


def forward_body(ins, outs, scratch, makers):
    ids, segments, padding, stream_hbm, cot_hbm, codebook, own_qkv, own_out, own_up, own_down, norms = ins
    (
        attn_out,
        qkv_out,
        out_weight_out,
        cot_full,
        inputs_share,
        gains,
        mask,
        projected,
        attended,
        middle,
        ffn_full,
        up_full,
        down_full,
    ) = outs
    (
        everyone,
        norm_tile,
        other_segments,
        other_padding,
        chunk,
        total,
        stream,
        cot_half,
        halves,
        attn_in,
        weight,
        out_weight,
        tokens,
        ffn_share,
        load_sem,
        swap_send,
        swap_recv,
    ) = scratch
    make_small, make_qkv, make_out, make_up, make_down, make_cot, make_attn, make_heads, make_share = makers
    ylo, x, z, yhi, core = place()
    small = make_small(norm_tile, everyone)
    qkv = make_qkv(own_qkv, weight)
    out = make_out(own_out, out_weight.at[core])
    up, down = make_up(own_up, up_full), make_down(own_down, down_full)
    cot_move = make_cot(cot_half, cot_full)
    attn_move = make_attn(halves, attn_in)
    heads = make_heads(attended, tokens)
    spread = make_share(ffn_share, ffn_full)

    def fetch(j):
        rows = pl.ds(j * CODE_CHUNK, CODE_CHUNK)
        return pltpu.make_async_copy(codebook.at[rows], chunk.at[j % 2], load_sem.at[j % 2])

    mine = pl.ds(pl.multiple_of(core * 256, 256), 256)
    loads = [fetched(stream_hbm.at[mine], stream, load_sem.at[2])]
    for u in range(2):
        rows = pl.ds(pl.multiple_of(core * 256 + u * SHARE, SHARE), SHARE)
        loads.append(fetched(cot_hbm.at[rows], cot_half.at[0, u], load_sem.at[3 + u]))
    fetch(0).start()
    lane = lax.broadcasted_iota(jnp.int32, (8, 128), 1)
    norm_tile[...] = jnp.where(lax.div(lane, 64) == lax.rem(z, 2), norms[...].astype(f32), 0.0)
    step(small, qkv, out)
    row_swaps = [
        remote(segments, other_segments, swap_send.at[0], swap_recv.at[0], lo_partner()),
        remote(padding, other_padding, swap_send.at[1], swap_recv.at[1], lo_partner()),
    ]
    for swap in row_swaps:
        swap.start()
    for load in loads:
        load.wait()
    step(cot_move)
    total[...] = stream[...].astype(f32)
    my_ids = ids[:, mine]
    count = CODES // CODE_CHUNK
    for j in range(count):
        if j + 1 < count:
            fetch(j + 1).start()
        fetch(j).wait()
        code = lax.broadcasted_iota(jnp.int32, (CODE_CHUNK, 256), 0) + j * CODE_CHUNK
        pick = jnp.where(my_ids == code, 1.0, 0.0).astype(bf16)
        for part in range(2):
            columns = pl.ds(part * 1024, 1024)
            total[:, columns] += outer_dot(pick, chunk[j % 2, :, columns])
        step((qkv, out, qkv, out)[j])
    step(small)
    for t in range(16):
        pair = everyone[2 * t, pl.ds(0, 8)] + everyone[2 * t + 1, pl.ds(0, 8)]
        gains[:, pl.ds(128 * t, 128)] = pair
    gain, shift = gains[pl.ds(0, 1)], gains[pl.ds(1, 1)]
    for u in range(2):

        def norm(rows):
            value = total[pl.ds(pl.multiple_of(u * SHARE + rows.start, 32), 32)]
            normed, _ = standardize(value)
            halves[0, u, rows] = (normed * gain + shift).astype(bf16)

        some_rows(SHARE, 32, norm)
    step(attn_move, qkv, out)

    def keep(rows):
        inputs_share[rows] = total[pl.ds(pl.multiple_of(yhi * SHARE + rows.start, 32), 32)]

    some_rows(SHARE, 32, keep)
    step(qkv, qkv)

    def see(r, segment_row, padding_row):
        turned = jnp.broadcast_to(segment_row.astype(f32), (SHARE, 512)).T[:, 0:1]
        query = lax.broadcasted_iota(jnp.int32, (512, 512), 0)
        key = lax.broadcasted_iota(jnp.int32, (512, 512), 1)
        same = turned == segment_row.astype(f32)
        live = (padding_row == 1) | (query == key)
        mask[r] = jnp.where(same & live & (key <= query), 1.0, 0.0).astype(bf16)

    for swap in row_swaps:
        swap.wait()
    see(ylo, segments[...], padding[...])
    see(1 - ylo, other_segments[...], other_padding[...])
    step(qkv, cot_move, qkv, out, out)
    step(attn_move)
    finish(qkv)
    step(out, out, up)
    finish(cot_move, attn_move)
    writes = [
        fetched(attn_in, attn_out, load_sem.at[0]),
        fetched(weight, qkv_out, load_sem.at[1]),
    ]

    def project(r):
        rows = attn_in[0, r].reshape(512, WIDTH)
        for t in range(3):
            columns = pl.ds(t * 256, 256)
            part = weight[:, :, :, :, columns].reshape(WIDTH, 256)
            projected[r, :, columns] = dot(rows, part).astype(bf16)

    def attend(r):
        for h in range(2):
            key = projected[r, :, pl.ds(256 + h * HEAD, HEAD)]
            value = projected[r, :, pl.ds(512 + h * HEAD, HEAD)]
            for c in range(2):
                rows = pl.ds(c * 256, 256)
                query = projected[r, rows, pl.ds(h * HEAD, HEAD)]
                scores = turned_dot(query, key) * HEAD ** (-0.5)
                scores = jnp.where(mask[r, rows].astype(f32) > 0.5, scores, masked_score)
                expd = jnp.exp(scores - jnp.max(scores, axis=-1, keepdims=True))
                probs = expd / jnp.sum(expd, axis=-1, keepdims=True)
                result = dot(probs.astype(bf16), value).astype(bf16)
                for u in range(2):
                    attended[r, c, u, :, pl.ds(h * HEAD, HEAD)] = result[u * SHARE : (u + 1) * SHARE]

    project(1 - ylo)
    step(out, down)
    attend(1 - ylo)
    step(heads)
    step(out, up)
    project(ylo)
    finish(out)
    swap = remote(
        out_weight.at[core], out_weight.at[core], swap_send.at[2], swap_recv.at[2], core_partner()
    )
    swap.start()
    step(down)
    attend(ylo)
    step(heads)
    step(up, down)
    finish(heads)
    there = out_weight.at[1 - core]
    remote(there, there, swap_send.at[2], swap_recv.at[2], core_partner()).wait_recv()
    writes.append(fetched(out_weight, out_weight_out, load_sem.at[2]))

    def branch(n, carry):
        columns = pl.ds(pl.multiple_of(n * 256, 256), 256)
        value = inputs_share[:, columns]
        for c in range(2):
            for h in range(2):
                features = pl.ds((h * 2 + c) * 512, 512)
                part = out_weight[c, h * 2 + lax.div(n, 4), lax.rem(n, 4)].reshape(256, 512)
                value += turned_dot(tokens[:, features], part)
        middle[:, columns] = value
        return carry

    lax.fori_loop(0, WIDTH // 256, branch, 0)
    gain_two, shift_two = gains[pl.ds(2, 1)], gains[pl.ds(3, 1)]

    def norm_two(rows):
        normed, _ = standardize(middle[rows])
        ffn_share[rows] = (normed * gain_two + shift_two).astype(bf16)

    some_rows(SHARE, 32, norm_two)
    step(spread)
    step(up, down)
    step(up, down)
    step(up, down)
    step(spread)
    step(up, down)
    step(spread)
    step(up, down)
    finish(spread, up, down)
    for write in writes:
        write.wait()
    swap.wait_send()


def forward(ids, segments, padding, stream, cot, codebook, own_qkv, own_out, own_up, own_down, norms):
    tokens_full = (shaped(bf16, 1, 2, 2, 2, SHARE, WIDTH), ANY)
    return kernel_call(
        forward_body,
        [
            small_gather(),
            weight_gather(768),
            weight_gather(512, spread=True),
            weight_gather(PART, flat=True),
            weight_gather(PART, flat=True),
            row_exchange(),
            row_exchange(),
            heads_to_tokens(),
            share_gather(),
        ],
        DP + GROUP,
        [
            (ids, VMEM),
            (segments, VMEM),
            (padding, VMEM),
            (stream, ANY),
            (cot, ANY),
            (codebook, ANY),
            (own_qkv, VMEM),
            (own_out, VMEM),
            (own_up, VMEM),
            (own_down, VMEM),
            (norms, VMEM),
        ],
        [
            tokens_full,
            gathered(768),
            (shaped(bf16, 2, 4, 4, 4, 64, 512), ANY),
            tokens_full,
            (shaped(f32, SHARE, WIDTH), VMEM),
            (shaped(f32, 8, WIDTH), VMEM),
            (shaped(bf16, 2, 512, 512), VMEM),
            (shaped(bf16, 2, 512, 768), VMEM),
            (shaped(bf16, 2, 2, 2, SHARE, 256), VMEM),
            (shaped(f32, SHARE, WIDTH), VMEM),
            (shaped(bf16, 2, 2, 2, SHARE, WIDTH), ANY),
            gathered(PART),
            gathered(PART),
        ],
        [
            pltpu.VMEM((32, 8, 128), f32),
            pltpu.VMEM((8, 128), f32),
            pltpu.VMEM((1, 512), jnp.int32),
            pltpu.VMEM((1, 512), jnp.int32),
            pltpu.VMEM((2, CODE_CHUNK, WIDTH), bf16),
            pltpu.VMEM((256, WIDTH), f32),
            pltpu.VMEM((256, WIDTH), bf16),
            pltpu.VMEM((1, 2, SHARE, WIDTH), bf16),
            pltpu.VMEM((1, 2, SHARE, WIDTH), bf16),
            pltpu.VMEM((1, 2, 2, 2, SHARE, WIDTH), bf16),
            pltpu.VMEM((2, 4, 4, 64, 768), bf16),
            pltpu.VMEM((2, 4, 4, 4, 64, 512), bf16),
            pltpu.VMEM((SHARE, WIDTH), bf16),
            pltpu.VMEM((SHARE, WIDTH), bf16),
            sems(5),
            sems(3),
            sems(3),
        ],
        0,
    )


SLOPE = 0.7978845608028654
CUBIC = 0.044715


def ffn_body(ins, outs, scratch, makers):
    ffn_hbm, cot_hbm, up_hbm, down_hbm, middle, gains = ins
    sum_down, grad_down_rest, grad_up_weight, layer_out, grad_middle, small = outs
    (
        ffn_in,
        cot,
        up_weight,
        down_weight,
        hidden,
        grad_up,
        back,
        ahead,
        grad_down_weight,
        back_share,
        ahead_share,
        load_sem,
    ) = scratch
    make_back, make_ahead, make_down = makers
    ylo, x, z, yhi, core = place()
    back_sum = make_back(back, back_share)
    ahead_sum = make_ahead(ahead, ahead_share)
    down_sum = make_down(grad_down_weight, sum_down)
    own, partner = (pl.ds(pl.multiple_of(r * 512, 512), 512) for r in (ylo, 1 - ylo))
    loads = [
        fetched(ffn_hbm.at[own], ffn_in.at[own], load_sem.at[0]),
        fetched(up_hbm, up_weight, load_sem.at[1]),
        fetched(cot_hbm.at[own], cot.at[own], load_sem.at[2]),
        fetched(down_hbm, down_weight, load_sem.at[3]),
        fetched(ffn_hbm.at[partner], ffn_in.at[partner], load_sem.at[4]),
        fetched(cot_hbm.at[partner], cot.at[partner], load_sem.at[5]),
    ]

    def units(rows):
        def one(n, carry):
            columns = pl.ds(pl.multiple_of(n * 512, 512), 512)
            value = dot(ffn_in[rows], up_weight[:, columns])
            grad = dot(cot[rows], down_weight[:, columns])
            square = value * value
            bend = jnp.tanh(SLOPE * value * (1.0 + CUBIC * square))
            half = 0.5 * (1.0 + bend)
            hidden[rows, columns] = (value * half).astype(bf16)
            slope = half + 0.5 * value * (1.0 - bend * bend) * SLOPE * (1.0 + 3.0 * CUBIC * square)
            grad_up[rows, columns] = (grad * slope).astype(bf16)
            return carry

        lax.fori_loop(0, PART // 512, one, 0)

    def spread_out(r, rows, source, weight, target):
        def one(n, carry):
            columns = pl.ds(pl.multiple_of(n * 512, 512), 512)
            value = turned_dot(source[rows], weight[columns]).astype(bf16)
            for c in range(2):
                for u in range(2):
                    at = (2 * c + u) * SHARE
                    target[r, c, u, :, columns] = value[at : at + SHARE]
            return carry

        lax.fori_loop(0, WIDTH // 512, one, 0)

    def weight_grad(left, right, target):
        def one(n, carry):
            columns = pl.ds(pl.multiple_of(n * 256, 256), 256)
            value = outer_dot(left[:, columns], right[...]).astype(bf16)
            for j in range(4):
                target[lax.div(n, 4), lax.rem(n, 4), j] = value[64 * j : 64 * j + 64]
            return carry

        lax.fori_loop(0, WIDTH // 256, one, 0)

    near, rest = pl.ds(0, 512), pl.ds(512, 512)
    for load in loads[:4]:
        load.wait()
    units(own)
    spread_out(ylo, own, grad_up, up_weight, back)
    step(back_sum)
    for load in loads[4:]:
        load.wait()
    units(partner)
    step(back_sum)
    weight_grad(cot, hidden.at[:, near], grad_down_weight)
    step(down_sum)
    spread_out(1 - ylo, partner, grad_up, up_weight, back)
    step(back_sum)
    spread_out(ylo, own, hidden, down_weight, ahead)
    step(back_sum)
    step(ahead_sum)
    step(down_sum)
    spread_out(1 - ylo, partner, hidden, down_weight, ahead)
    step(ahead_sum, ahead_sum)
    step(down_sum)
    weight_grad(cot, hidden.at[:, rest], grad_down_rest)
    step(down_sum)
    step(ahead_sum)
    weight_grad(ffn_in, grad_up, grad_up_weight)
    step(down_sum)
    finish(back_sum)
    gain = gains[pl.ds(2, 1)]
    small[...] = jnp.zeros_like(small)

    def back_norm(i, carry):
        at = pl.multiple_of(i * 32, 32)
        rows = pl.ds(at, 32)
        normed, inverse = standardize(middle[rows])
        value, grad_gain, grad_shift = norm_back(back_share[rows], normed, inverse, gain)
        here = pl.multiple_of(ylo * 512 + core * 256 + yhi * SHARE + at, 32)
        grad_middle[rows] = value + cot[pl.ds(here, 32)].astype(f32)
        small[pl.ds(2, 1)] += grad_gain
        small[pl.ds(3, 1)] += grad_shift
        return carry

    lax.fori_loop(0, SHARE // 32, back_norm, 0)
    step(down_sum, down_sum)
    finish(ahead_sum)

    def end(rows):
        layer_out[0, rows] = (middle[rows] + ahead_share[rows]).astype(bf16)

    some_rows(SHARE, 16, end)
    finish(down_sum)


def feed_forward(ffn_in, cot, up, down, middle, gains):
    return kernel_call(
        ffn_body,
        [share_sum(), share_sum(), weight_sum(512)],
        XZ + ["y1", "y2", "y3", "core"],
        [(ffn_in, ANY), (cot, ANY), (up, ANY), (down, ANY), (middle, VMEM), (gains, VMEM)],
        [
            (shaped(bf16, 2, 64, 512), VMEM),
            (shaped(bf16, 2, 4, 4, 64, 512), VMEM),
            (shaped(bf16, 2, 4, 4, 64, PART), VMEM),
            (shaped(bf16, 1, SHARE, WIDTH), VMEM),
            (shaped(f32, SHARE, WIDTH), VMEM),
            (shaped(f32, 8, WIDTH), VMEM),
        ],
        [
            pltpu.VMEM((1024, WIDTH), bf16),
            pltpu.VMEM((1024, WIDTH), bf16),
            pltpu.VMEM((WIDTH, PART), bf16),
            pltpu.VMEM((WIDTH, PART), bf16),
            pltpu.VMEM((1024, PART), bf16),
            pltpu.VMEM((1024, PART), bf16),
            pltpu.VMEM((2, 2, 2, SHARE, WIDTH), bf16),
            pltpu.VMEM((2, 2, 2, SHARE, WIDTH), bf16),
            pltpu.VMEM((2, 4, 4, 64, 512), bf16),
            pltpu.VMEM((SHARE, WIDTH), f32),
            pltpu.VMEM((SHARE, WIDTH), f32),
            sems(6),
        ],
        2,
        62,
    )


def back_body(ins, outs, scratch, makers):
    (
        attn_hbm,
        weight_hbm,
        out_hbm,
        down_hbm,
        up_hbm,
        projected,
        attended,
        mask,
        grad_middle,
        inputs_share,
        layer_out,
        small_in,
        gains,
    ) = ins
    layer_full, input_full, sum_down, sum_up, sum_qkv, sum_out, small_out, branch_full = outs
    (
        attn_in,
        weight,
        out_weight,
        grad_down_weight,
        grad_up_weight,
        grad_qkv_weight,
        grad_out_weight,
        grad_branch,
        branch_share,
        grad_tokens,
        grad_heads,
        grad_projected,
        back,
        back_share,
        input_share,
        small,
        load_sem,
    ) = scratch
    make_down, make_up, make_qkv, make_out, make_heads, make_branch, make_back, make_layer, make_input, make_small = makers
    ylo, x, z, yhi, core = place()
    down_sum = make_down(grad_down_weight, sum_down)
    up_sum = make_up(grad_up_weight, sum_up)
    qkv_sum = make_qkv(grad_qkv_weight, sum_qkv)
    out_sum = make_out(grad_out_weight, sum_out)
    heads = make_heads(grad_tokens, grad_heads)
    branch = make_branch(branch_share, branch_full)
    back_sum = make_back(back, back_share)
    layer_move = make_layer(layer_out, layer_full)
    input_move = make_input(input_share, input_full)
    small_sum = make_small(small, small_out)
    loads = [
        fetched(out_hbm, out_weight, load_sem.at[0]),
        fetched(down_hbm, grad_down_weight, load_sem.at[1]),
        fetched(up_hbm, grad_up_weight, load_sem.at[2]),
        fetched(weight_hbm, weight, load_sem.at[3]),
        fetched(attn_hbm, attn_in, load_sem.at[4]),
    ]

    def low(rows):
        branch_share[rows] = grad_middle[rows].astype(bf16)

    step(layer_move)
    some_rows(SHARE, 32, low)
    loads[0].wait()
    for h in range(2):
        for c in range(2):
            grad_tokens[:, pl.ds((h * 2 + c) * 512, 512)] = dot(
                branch_share[...], out_weight[c, h]
            ).astype(bf16)
    step(heads)
    step(branch)
    loads[1].wait()
    step(down_sum)
    loads[2].wait()
    step(up_sum)
    step(layer_move)
    finish(heads)

    def attend(r):
        for h in range(2):
            query = projected[r, :, pl.ds(h * HEAD, HEAD)]
            key = projected[r, :, pl.ds(256 + h * HEAD, HEAD)]
            value = projected[r, :, pl.ds(512 + h * HEAD, HEAD)]
            grad = grad_heads[r, :, :, :, pl.ds(h * HEAD, HEAD)].reshape(512, HEAD)
            scores = turned_dot(query, key) * HEAD ** (-0.5)
            scores = jnp.where(mask[r].astype(f32) > 0.5, scores, masked_score)
            expd = jnp.exp(scores - jnp.max(scores, axis=-1, keepdims=True))
            probs = expd / jnp.sum(expd, axis=-1, keepdims=True)
            grad_probs = turned_dot(grad, value)
            inner = jnp.sum(grad_probs * probs, axis=-1, keepdims=True)
            grad_scores = (probs * (grad_probs - inner)).astype(bf16)
            parts = (
                dot(grad_scores, key) * HEAD ** (-0.5),
                outer_dot(grad_scores, query) * HEAD ** (-0.5),
                outer_dot(probs.astype(bf16), grad),
            )
            for t in range(3):
                grad_projected[pl.ds(pl.multiple_of(r * 512, 512), 512), pl.ds(t * 256 + h * HEAD, HEAD)] = parts[
                    t
                ].astype(bf16)

    def spread_out(r):
        def one(n, carry):
            columns = pl.ds(pl.multiple_of(n * 512, 512), 512)
            rows = pl.ds(pl.multiple_of(r * 512, 512), 512)
            value = turned_dot(grad_projected[rows], weight[columns]).astype(bf16)
            for c in range(2):
                for u in range(2):
                    at = (2 * c + u) * SHARE
                    back[r, c, u, :, columns] = value[at : at + SHARE]
            return carry

        lax.fori_loop(0, WIDTH // 512, one, 0)

    def weight_grad(left, right, target):
        def one(n, carry):
            columns = pl.ds(pl.multiple_of(n * 256, 256), 256)
            value = outer_dot(left[..., columns].reshape(1024, 256), right).astype(bf16)
            for j in range(4):
                target[lax.div(n, 4), lax.rem(n, 4), j] = value[64 * j : 64 * j + 64]
            return carry

        lax.fori_loop(0, WIDTH // 256, one, 0)

    attend(ylo)
    step(down_sum)
    loads[3].wait()
    spread_out(ylo)
    step(back_sum)
    step(down_sum)
    attend(1 - ylo)
    step(back_sum)
    step(branch)
    spread_out(1 - ylo)
    step(back_sum)
    step(up_sum)
    loads[4].wait()
    weight_grad(attn_in, grad_projected[...], grad_qkv_weight)
    step(back_sum)
    step(qkv_sum)
    step(down_sum, down_sum, up_sum, down_sum, down_sum)
    finish(branch)
    gather_load = fetched(branch_full, grad_branch, load_sem.at[5])
    step(up_sum)
    gather_load.wait()
    weight_grad(grad_branch, attended[...].reshape(1024, 256), grad_out_weight)
    step(out_sum)
    step(up_sum)
    finish(back_sum)
    gain = gains[pl.ds(0, 1)]
    small[...] = small_in[...]

    def back_norm(i, carry):
        rows = pl.ds(pl.multiple_of(i * 32, 32), 32)
        normed, inverse = standardize(inputs_share[rows])
        value, grad_gain, grad_shift = norm_back(back_share[rows], normed, inverse, gain)
        input_share[0, rows] = (grad_middle[rows] + value).astype(bf16)
        small[pl.ds(0, 1)] += grad_gain
        small[pl.ds(1, 1)] += grad_shift
        return carry

    lax.fori_loop(0, SHARE // 32, back_norm, 0)
    step(input_move, small_sum)
    step(qkv_sum, qkv_sum, up_sum, out_sum, out_sum)
    step(small_sum)
    step(up_sum, qkv_sum, qkv_sum, out_sum, out_sum)
    step(input_move)
    step(qkv_sum, out_sum, qkv_sum, out_sum)
    finish(layer_move, input_move, small_sum, down_sum, up_sum, qkv_sum, out_sum)


def attention_back(
    attn_in,
    weight,
    out_weight,
    grad_down_weight,
    grad_up_weight,
    projected,
    attended,
    mask,
    grad_middle,
    inputs_share,
    layer_out,
    small,
    gains,
):
    return kernel_call(
        back_body,
        [
            weight_sum(512),
            weight_sum(),
            weight_sum(768),
            weight_sum(256),
            tokens_to_heads(),
            share_gather(),
            share_sum(),
            row_gather(),
            row_gather(),
            small_reduce(),
        ],
        DP + MP + GROUP,
        [
            (attn_in, ANY),
            (weight, ANY),
            (out_weight, ANY),
            (grad_down_weight, ANY),
            (grad_up_weight, ANY),
            (projected, VMEM),
            (attended, VMEM),
            (mask, VMEM),
            (grad_middle, VMEM),
            (inputs_share, VMEM),
            (layer_out, VMEM),
            (small, VMEM),
            (gains, VMEM),
        ],
        [
            (shaped(bf16, 1, 2, 2, SHARE, WIDTH), ANY),
            (shaped(bf16, 1, 2, 2, SHARE, WIDTH), ANY),
            (shaped(bf16, 2, 64, 512), VMEM),
            (shaped(bf16, 2, 64, PART), VMEM),
            (shaped(bf16, 2, 64, 768), VMEM),
            (shaped(bf16, 2, 64, 256), VMEM),
            (shaped(f32, 8, 128), VMEM),
            (shaped(bf16, 2, 2, 2, SHARE, WIDTH), ANY),
        ],
        [
            pltpu.VMEM((1024, WIDTH), bf16),
            pltpu.VMEM((WIDTH, 768), bf16),
            pltpu.VMEM((2, 2, WIDTH, 512), bf16),
            pltpu.VMEM((2, 4, 4, 64, 512), bf16),
            pltpu.VMEM((2, 4, 4, 64, PART), bf16),
            pltpu.VMEM((2, 4, 4, 64, 768), bf16),
            pltpu.VMEM((2, 4, 4, 64, 256), bf16),
            pltpu.VMEM((2, 2, 2, SHARE, WIDTH), bf16),
            pltpu.VMEM((SHARE, WIDTH), bf16),
            pltpu.VMEM((SHARE, WIDTH), bf16),
            pltpu.VMEM((2, 2, 2, SHARE, 256), bf16),
            pltpu.VMEM((1024, 768), bf16),
            pltpu.VMEM((2, 2, 2, SHARE, WIDTH), bf16),
            pltpu.VMEM((SHARE, WIDTH), f32),
            pltpu.VMEM((1, SHARE, WIDTH), bf16),
            pltpu.VMEM((8, WIDTH), f32),
            sems(6),
        ],
        3,
        62,
    )


def on_device(
    stream,
    code_ids,
    segment_ids,
    padding,
    codebook,
    norm1_gain,
    norm1_shift,
    w_qkv,
    w_out,
    norm2_gain,
    norm2_shift,
    w_up,
    w_down,
    cotangent,
):
    ylo, x, z, yhi, core = place()
    own_qkv = w_qkv.reshape(64, 3, 2, 256).transpose(2, 0, 1, 3).reshape(2, 64, 768)
    norms = jnp.stack([norm1_gain, norm1_shift, norm2_gain, norm2_shift] * 2)
    norms = jnp.concatenate([norms, norms], axis=1)
    (
        attn_in,
        qkv_full,
        out_full,
        cot,
        inputs_share,
        gains,
        allowed,
        projected,
        attended,
        middle,
        ffn_in,
        up_full,
        down_full,
    ) = forward(
        code_ids,
        segment_ids,
        padding,
        stream[0],
        cotangent[0],
        codebook,
        own_qkv,
        w_out,
        w_up,
        w_down,
        norms,
    )
    sum_down, grad_down_rest, grad_up_weight, layer_out, grad_middle, small = feed_forward(
        ffn_in.reshape(1024, WIDTH),
        cot.reshape(1024, WIDTH),
        up_full.reshape(WIDTH, PART),
        down_full.reshape(WIDTH, PART),
        middle,
        gains,
    )
    layer_out, input_grad, sum_down_rest, sum_up, sum_qkv, sum_out, small, _ = attention_back(
        attn_in.reshape(1024, WIDTH),
        qkv_full.reshape(WIDTH, 768),
        out_full.reshape(2, 2, WIDTH, 512),
        grad_down_rest,
        grad_up_weight,
        projected,
        attended,
        allowed,
        grad_middle,
        inputs_share,
        layer_out,
        small,
        gains,
    )

    sum_down = jnp.concatenate([sum_down, sum_down_rest], axis=2)
    sum_qkv, sum_out, sum_up, sum_down = (g.astype(f32) for g in (sum_qkv, sum_out, sum_up, sum_down))
    out_qkv = sum_qkv.reshape(2, 64, 3, 256).transpose(1, 2, 0, 3).reshape(64, 3, 512)
    out_out = sum_out.transpose(1, 0, 2).reshape(64, 512)
    out_up = sum_up.transpose(1, 0, 2).reshape(64, WIDTH)
    out_down = sum_down.transpose(1, 0, 2).reshape(64, WIDTH)
    odd = lax.rem(z, 2) == 1
    small = jnp.where(odd, small[:4, 64:], small[:4, :64])
    return (
        layer_out.reshape(1, 512, WIDTH).astype(f32),
        input_grad.reshape(1, 512, WIDTH).astype(f32),
        small[0],
        small[1],
        out_qkv,
        out_out,
        small[2],
        small[3],
        out_up,
        out_down,
    )


def solution(mesh):
    in_specs = (
        P("dp", None, None),
        P("dp", None),
        P("dp", None),
        P("dp", None),
        P(),
        P("dp"),
        P("dp"),
        P("dp", None, "mp"),
        P("dp", "mp"),
        P("dp"),
        P("dp"),
        P("dp", "mp"),
        P("dp", "mp"),
        P("dp", None, None),
    )
    out_specs = (
        P("dp", None, None),
        P("dp", None, None),
        P("dp"),
        P("dp"),
        P("dp", None, "mp"),
        P("dp", "mp"),
        P("dp"),
        P("dp"),
        P("dp", "mp"),
        P("dp", "mp"),
    )
    return jax.shard_map(
        on_device, mesh=mesh, in_specs=in_specs, out_specs=out_specs, check_vma=False
    )
```

profile of v0, /device:TPU:16, one launch (start us, length us, event | category | flops | bytes accessed | tf_op | source)
XLA Modules:
  0.0 299.2 jit_solution(14946856730200767530)
XLA Ops:
  0.6 1.0 reshape.105
  1.6 0.2 copy.39
  1.8 0.9 reshape.106.refs_6_
  2.7 0.8 stack.23
  3.5 0.7 pad_maximum_fusion.refs_10_
  4.1 105.8 %shard_map.213 = (bf16[1,2,2,2,128,2048]{5,4,3,2,1,0:T(8,128)(2,1)}, bf16[2,4,4,64,768]{4,3,2,1,0:T(8,128)(2,1)}, bf16[2,4,4,4,64,512]{5,4,3,2,1,0:T(8,128)(2,1)...) custom-call(s32[1,512]{1,0:T(1,128)} %refs_0_.1, ...), custom_call_target="tpu_custom_call" | custom-call | tf_op jit(solution)/shard_map/pallas_call | solution.py:135
  109.9 73.2 %shard_map.214 = (bf16[2,64,512]{2,1,0:T(8,128)(2,1)}, bf16[2,4,4,64,512]{4,3,2,1,0:T(8,128)(2,1)}, bf16[2,4,4,64,1024]{4,3,2,1,0:T(8,128)(2,1)}, bf16[1,128,204...) custom-call(bf16[1024,2048]{1,0:T(8,128)(2,1)} %bitcast.49, bf16[1024,2048]{1,0:T(8,128)(2,1)} %bitcast.48, ...), custom_call_target="tpu_custom_call" | custom-call | tf_op jit(solution)/shard_map/pallas_call | solution.py:135
  183.1 0.0 copy-start.2
  183.1 103.6 %shard_map.215 = (bf16[1,2,2,128,2048]{4,3,2,1,0:T(8,128)(2,1)}, bf16[1,2,2,128,2048]{4,3,2,1,0:T(8,128)(2,1)}, bf16[2,64,512]{2,1,0:T(8,128)(2,1)}, bf16[2,64,1...) custom-call(bf16[1024,2048]{1,0:T(8,128)(2,1)} %bitcast.52, ...), custom_call_target="tpu_custom_call" | custom-call | tf_op jit(solution)/shard_map/pallas_call | solution.py:135
  286.8 0.0 copy-start
  286.8 0.0 copy-done.2
  286.8 1.3 convert_bitcast_fusion
  288.1 0.8 copy.36
  288.9 0.8 copy.37
  289.7 0.0 copy-done
  289.7 0.0 copy-start.1
  289.7 0.0 copy-start.3
  289.7 0.0 copy-start.4
  289.8 6.1 %bitcast_convert_fusion = (f32[1,512,2048]{2,1,0:T(8,128)}, f32[1,512,2048]{2,1,0:T(8,128)}) fusion(bf16[1,2,2,128,2048]{4,3,2,1,0:T(8,128)(2,1)} %get-tuple-element.55, bf16[1,2,2,128,2048]{4,3,2,1,0:T(8,128)(2,1)S(1)} %copy-done), kind=kLoop, calls=%fused_computation | loop fusion | flops 2097152 | bytes 12582912 | tf_op jit(solution)/shard_map/convert_element_type | solution.py:1570
  295.9 0.0 copy-done.1
  295.9 0.2 reshape.138
  296.1 0.3 copy.31
  296.4 1.1 reshape.126
  297.4 0.0 copy-done.3
  297.5 0.7 copy.35
  298.1 0.0 copy-done.4
  298.1 0.1 slice_select_fusion
  298.2 0.5 slice_bitcast_fusion
  (1 shorter events, 0.0 us)
Async XLA Ops:
  183.1 103.7 %copy-start.2 = (bf16[2,64,512]{2,1,0:T(8,128)(2,1)S(1)}, bf16[2,64,512]{2,1,0:T(8,128)(2,1)}, u32[]{:S(2)}) copy-start(bf16[2,64,512]{2,1,0:T(8,128)(2,1)} %get-tuple-element.60) | copy-start | bytes 393220
  286.8 3.0 copy-start
  289.7 6.1 %copy-start.1 = (bf16[2,64,768]{2,1,0:T(8,128)(2,1)S(1)}, bf16[2,64,768]{2,1,0:T(8,128)(2,1)}, u32[]{:S(2)}) copy-start(bf16[2,64,768]{2,1,0:T(8,128)(2,1)} %get-tuple-element.57) | copy-start | bytes 589828
  289.7 7.7 %copy-start.3 = (bf16[2,64,256]{2,1,0:T(8,128)(2,1)S(1)}, bf16[2,64,256]{2,1,0:T(8,128)(2,1)}, u32[]{:S(2)}) copy-start(bf16[2,64,256]{2,1,0:T(8,128)(2,1)} %get-tuple-element.58) | copy-start | bytes 196612
  289.7 8.4 %copy-start.4 = (f32[8,128]{1,0:T(8,128)S(1)}, f32[8,128]{1,0:T(8,128)}, u32[]{:S(2)}) copy-start(f32[8,128]{1,0:T(8,128)} %get-tuple-element.56) | copy-start | bytes 12292
where the time goes:
time: 304 us; the launch traced here: 299 us
  Pallas kernels  283 us (93%)
  other arithmetic  8.11 us (3%)
  local copies, waits for them, and re-layouts  7.31 us (2%)
    pallas_call x3, Pallas kernels, kernel_call(): pl.pallas_call(kernel, out_shape=[shape for shape, _ in outs], in_specs=[...  283 us
    convert_element_type x1, other arithmetic, on_device(): input_grad.reshape(1, 512, WIDTH).astype(f32)  6.1 us

commit v1 on v0

--- a/solution.py
+++ b/solution.py
@@ -58,7 +58,7 @@
     barrier = pltpu.get_barrier_semaphore()
     for peer in peers:
         pl.semaphore_signal(barrier, inc=1, device_id=peer, device_id_type=MESH)
-    pl.semaphore_wait(barrier, len(peers))
+    return lambda: pl.semaphore_wait(barrier, len(peers))
 
 
 def remote(src, dst, send_sem, recv_sem, peer):
@@ -88,31 +88,21 @@
     "x-": lambda: xz_neighbour(0, -1),
     "z+": lambda: xz_neighbour(1, 1),
     "z-": lambda: xz_neighbour(1, -1),
+    "x2": lambda: xz_neighbour(0, 2),
+    "z2": lambda: xz_neighbour(1, 2),
     "y1": lambda: y_peer(1),
     "y2": lambda: y_peer(2),
     "y3": lambda: y_peer(3),
 }
 
 
-def dp_peer(step):
-    return (lax.rem(lax.axis_index("dp") + step, 32), lax.axis_index("mp"))
-
-
 def diagonal_peer(step):
     dp, mp = y_peer(step)
     return (dp, mp + 1 - 2 * lax.rem(mp, 2))
 
 
-def mp_peer(step):
-    return (lax.axis_index("dp"), lax.rem(lax.axis_index("mp") + step, 4))
-
-
-PEERS.update({f"dp{k}": functools.partial(dp_peer, k) for k in range(1, 32)})
-PEERS.update({f"mp{k}": functools.partial(mp_peer, k) for k in range(1, 4)})
 PEERS.update({f"d{k}": functools.partial(diagonal_peer, k) for k in range(1, 4)})
 GROUP = ["y1", "y2", "y3", "core", "d1", "d2", "d3"]
-DP = [f"dp{k}" for k in range(1, 32)]
-MP = ["mp1", "mp2", "mp3"]
 
 
 def kernel_call(body, jobs, peers, ins, outs, scratch, collective_id, mib=56):
@@ -129,8 +119,8 @@
         for job in jobs:
             own = take(len(job["scratch"]))
             makers.append(lambda *given, job=job, own=own: job["steps"](*given, *own))
-        greet([PEERS[name]() for name in peers])
-        body(*groups, makers)
+        ready = greet([PEERS[name]() for name in peers])
+        body(*groups, makers, ready)
 
     return pl.pallas_call(
         kernel,
@@ -159,71 +149,92 @@
 
 def small_gather():
     def steps(own, everyone, send, recv):
-        dp, mp = lax.axis_index("dp"), lax.axis_index("mp")
-
-        def move(k):
-            return remote(own, everyone.at[dp], send.at[k], recv.at[dp], dp_peer(k))
-
-        def start(k, carry):
-            move(k).start()
-            return carry
-
-        lax.fori_loop(1, 32, start, 0)
-        everyone[dp] = own[...]
-        yield
-
-        def end(k, carry):
-            source = lax.rem(dp + k, 32)
-            move(k).wait_send()
-            remote(own, everyone.at[source], send.at[k], recv.at[source], dp_peer(k)).wait_recv()
-            return carry
-
-        lax.fori_loop(1, 32, end, 0)
-
-    return {"scratch": [sems(32), sems(32)], "steps": steps}
+        ylo, x, z, yhi, core = place()
+        sent = []
+
+        def go(here, n, peer):
+            copy = remote(here, here, send.at[n], recv.at[n], peer)
+            copy.start()
+            sent.append(copy)
+
+        def came(here, n):
+            remote(here, here, send.at[n], recv.at[n], lo_partner()).wait_recv()
+
+        everyone[ylo, x, z] = own[...]
+        go(everyone.at[ylo, x, z], 0, lo_partner())
+        yield
+        came(everyone.at[1 - ylo, x, z], 0)
+        for k in (1, 2, 3):
+            go(everyone.at[:, x, z], k, xz_neighbour(0, k))
+        yield
+        for k in (1, 2, 3):
+            came(everyone.at[:, ring(x, -k), z], k)
+        for k in (1, 2, 3):
+            go(everyone.at[:, :, z], 3 + k, xz_neighbour(1, k))
+        yield
+        for k in (1, 2, 3):
+            came(everyone.at[:, :, ring(z, -k)], 3 + k)
+        for copy in sent:
+            copy.wait_send()
+
+    return {"scratch": [sems(7), sems(7)], "steps": steps}
 
 
 def small_reduce():
-    def steps(rows, out, arrived, summed, more, send, recv, send_two, recv_two):
-        dp = lax.axis_index("dp")
-
-        def move(k):
-            tile = lax.div(lax.rem(dp + k, 32), 2)
-            src = rows.at[:, pl.ds(pl.multiple_of(tile * 128, 128), 128)]
-            return remote(src, arrived.at[k], send.at[k], recv.at[k], dp_peer(k))
-
-        def start(k, carry):
-            move(k).start()
-            return carry
-
-        def add(k, total):
-            move(k).wait()
-            return total + arrived[k]
-
-        lax.fori_loop(1, 32, start, 0)
-        yield
-        mine = rows[:, pl.ds(pl.multiple_of(lax.div(dp, 2) * 128, 128), 128)]
-        summed[...] = lax.fori_loop(1, 32, add, mine)
-        copies = [
-            remote(summed, more.at[k - 1], send_two.at[k], recv_two.at[k], mp_peer(k))
-            for k in (1, 2, 3)
-        ]
-        for copy in copies:
+    def steps(rows, out, of_group, of_x, of_z, half, quarter, send, recv):
+        ylo, x, z, yhi, core = place()
+        y = yhi * 2 + ylo
+        waits = []
+
+        def go(src, dst, n, peer):
+            copy = remote(src, dst, send.at[n], recv.at[n], peer)
             copy.start()
-        yield
-        for copy in copies:
-            copy.wait()
-        out[...] = summed[...] + more[0] + more[1] + more[2]
+            waits.append(copy)
+
+        def lanes(start, size):
+            return pl.ds(pl.multiple_of(start, size), size)
+
+        for n, (k, flip) in enumerate(((1, 0), (1, 1), (2, 0), (2, 1), (3, 0), (3, 1), (0, 1))):
+            theirs = lanes(lax.rem(ring(y, k), 2) * 1024, 1024)
+            go(rows.at[:, theirs], of_group.at[n], n, diagonal_peer(k) if flip else y_peer(k))
+        yield
+        for copy in waits:
+            copy.wait_recv()
+        total = rows[:, lanes(ylo * 1024, 1024)]
+        for n in range(7):
+            total += of_group[n]
+        half[...] = total
+        for k in (1, 2, 3):
+            go(half.at[:, lanes(ring(x, k) * 256, 256)], of_x.at[k - 1], 6 + k, xz_neighbour(0, k))
+        yield
+        for copy in waits[7:]:
+            copy.wait_recv()
+        total = half[:, lanes(x * 256, 256)]
+        for n in range(3):
+            total += of_x[n]
+        quarter[...] = total
+        for k in (1, 2, 3):
+            theirs = lanes(lax.div(ring(z, k), 2) * 128, 128)
+            go(quarter.at[:, theirs], of_z.at[k - 1], 9 + k, xz_neighbour(1, k))
+        yield
+        for copy in waits[10:]:
+            copy.wait_recv()
+        total = quarter[:, lanes(lax.div(z, 2) * 128, 128)]
+        for n in range(3):
+            total += of_z[n]
+        out[...] = total
+        for copy in waits:
+            copy.wait_send()
 
     return {
         "scratch": [
-            pltpu.VMEM((32, 8, 128), f32),
-            pltpu.VMEM((8, 128), f32),
-            pltpu.VMEM((3, 8, 128), f32),
-            sems(32),
-            sems(32),
-            sems(4),
-            sems(4),
+            pltpu.VMEM((7, 4, 1024), f32),
+            pltpu.VMEM((3, 4, 256), f32),
+            pltpu.VMEM((3, 4, 128), f32),
+            pltpu.VMEM((4, 1024), f32),
+            pltpu.VMEM((4, 256), f32),
+            sems(13),
+            sems(13),
         ],
         "steps": steps,
     }
@@ -813,24 +824,29 @@
 CODE_CHUNK = 1024
 
 
-def forward_body(ins, outs, scratch, makers):
+def forward_body(ins, outs, scratch, makers, ready):
     ids, segments, padding, stream_hbm, cot_hbm, codebook, own_qkv, own_out, own_up, own_down, norms = ins
     (
         attn_out,
         qkv_out,
         out_weight_out,
         cot_full,
-        inputs_share,
+        inputs_out,
         gains,
-        mask,
-        projected,
-        attended,
-        middle,
+        mask_out,
+        projected_out,
+        attended_out,
+        middle_out,
         ffn_full,
         up_full,
         down_full,
     ) = outs
     (
+        inputs_share,
+        mask,
+        projected,
+        attended,
+        middle,
         everyone,
         norm_tile,
         other_segments,
@@ -872,6 +888,7 @@
     fetch(0).start()
     lane = lax.broadcasted_iota(jnp.int32, (8, 128), 1)
     norm_tile[...] = jnp.where(lax.div(lane, 64) == lax.rem(z, 2), norms[...].astype(f32), 0.0)
+    ready()
     step(small, qkv, out)
     row_swaps = [
         remote(segments, other_segments, swap_send.at[0], swap_recv.at[0], lo_partner()),
@@ -894,10 +911,11 @@
         for part in range(2):
             columns = pl.ds(part * 1024, 1024)
             total[:, columns] += outer_dot(pick, chunk[j % 2, :, columns])
-        step((qkv, out, qkv, out)[j])
-    step(small)
+        step(small, (qkv, out, qkv, out)[j])
+    finish(small)
     for t in range(16):
-        pair = everyone[2 * t, pl.ds(0, 8)] + everyone[2 * t + 1, pl.ds(0, 8)]
+        at = (t // 8, t // 2 % 4, t % 2 * 2)
+        pair = everyone[at] + everyone[at[0], at[1], at[2] + 1]
         gains[:, pl.ds(128 * t, 128)] = pair
     gain, shift = gains[pl.ds(0, 1)], gains[pl.ds(1, 1)]
     for u in range(2):
@@ -936,6 +954,8 @@
     writes = [
         fetched(attn_in, attn_out, load_sem.at[0]),
         fetched(weight, qkv_out, load_sem.at[1]),
+        fetched(inputs_share, inputs_out, load_sem.at[2]),
+        fetched(mask, mask_out, load_sem.at[3]),
     ]
 
     def project(r):
@@ -978,7 +998,9 @@
     finish(heads)
     there = out_weight.at[1 - core]
     remote(there, there, swap_send.at[2], swap_recv.at[2], core_partner()).wait_recv()
-    writes.append(fetched(out_weight, out_weight_out, load_sem.at[2]))
+    writes.append(fetched(out_weight, out_weight_out, load_sem.at[4]))
+    writes.append(fetched(projected, projected_out, load_sem.at[5]))
+    writes.append(fetched(attended, attended_out, load_sem.at[6]))
 
     def branch(n, carry):
         columns = pl.ds(pl.multiple_of(n * 256, 256), 256)
@@ -1000,6 +1022,7 @@
 
     some_rows(SHARE, 32, norm_two)
     step(spread)
+    writes.append(fetched(middle, middle_out, load_sem.at[7]))
     step(up, down)
     step(up, down)
     step(up, down)
@@ -1028,7 +1051,7 @@
             heads_to_tokens(),
             share_gather(),
         ],
-        DP + GROUP,
+        XZ + ["x2", "z2"] + GROUP,
         [
             (ids, VMEM),
             (segments, VMEM),
@@ -1047,18 +1070,23 @@
             gathered(768),
             (shaped(bf16, 2, 4, 4, 4, 64, 512), ANY),
             tokens_full,
-            (shaped(f32, SHARE, WIDTH), VMEM),
+            (shaped(f32, SHARE, WIDTH), ANY),
             (shaped(f32, 8, WIDTH), VMEM),
-            (shaped(bf16, 2, 512, 512), VMEM),
-            (shaped(bf16, 2, 512, 768), VMEM),
-            (shaped(bf16, 2, 2, 2, SHARE, 256), VMEM),
-            (shaped(f32, SHARE, WIDTH), VMEM),
+            (shaped(bf16, 2, 512, 512), ANY),
+            (shaped(bf16, 2, 512, 768), ANY),
+            (shaped(bf16, 2, 2, 2, SHARE, 256), ANY),
+            (shaped(f32, SHARE, WIDTH), ANY),
             (shaped(bf16, 2, 2, 2, SHARE, WIDTH), ANY),
             gathered(PART),
             gathered(PART),
         ],
         [
-            pltpu.VMEM((32, 8, 128), f32),
+            pltpu.VMEM((SHARE, WIDTH), f32),
+            pltpu.VMEM((2, 512, 512), bf16),
+            pltpu.VMEM((2, 512, 768), bf16),
+            pltpu.VMEM((2, 2, 2, SHARE, 256), bf16),
+            pltpu.VMEM((SHARE, WIDTH), f32),
+            pltpu.VMEM((2, 4, 4, 8, 128), f32),
             pltpu.VMEM((8, 128), f32),
             pltpu.VMEM((1, 512), jnp.int32),
             pltpu.VMEM((1, 512), jnp.int32),
@@ -1072,7 +1100,7 @@
             pltpu.VMEM((2, 4, 4, 4, 64, 512), bf16),
             pltpu.VMEM((SHARE, WIDTH), bf16),
             pltpu.VMEM((SHARE, WIDTH), bf16),
-            sems(5),
+            sems(8),
             sems(3),
             sems(3),
         ],
@@ -1084,10 +1112,15 @@
 CUBIC = 0.044715
 
 
-def ffn_body(ins, outs, scratch, makers):
-    ffn_hbm, cot_hbm, up_hbm, down_hbm, middle, gains = ins
-    sum_down, grad_down_rest, grad_up_weight, layer_out, grad_middle, small = outs
+def ffn_body(ins, outs, scratch, makers, ready):
+    ffn_hbm, cot_hbm, up_hbm, down_hbm, middle_hbm, out_hbm, gains = ins
+    sum_down, grad_up_out, layer_full, grad_middle_out, small, branch_share, grad_heads = outs
     (
+        layer_out,
+        middle,
+        grad_up_weight,
+        grad_middle,
+        grad_tokens,
         ffn_in,
         cot,
         up_weight,
@@ -1101,32 +1134,42 @@
         ahead_share,
         load_sem,
     ) = scratch
-    make_back, make_ahead, make_down = makers
+    make_back, make_ahead, make_down, make_heads, make_layer = makers
     ylo, x, z, yhi, core = place()
     back_sum = make_back(back, back_share)
     ahead_sum = make_ahead(ahead, ahead_share)
     down_sum = make_down(grad_down_weight, sum_down)
+    heads = make_heads(grad_tokens, grad_heads)
+    layer_move = make_layer(layer_out, layer_full)
     own, partner = (pl.ds(pl.multiple_of(r * 512, 512), 512) for r in (ylo, 1 - ylo))
     loads = [
         fetched(ffn_hbm.at[own], ffn_in.at[own], load_sem.at[0]),
         fetched(up_hbm, up_weight, load_sem.at[1]),
-        fetched(cot_hbm.at[own], cot.at[own], load_sem.at[2]),
+        fetched(ffn_hbm.at[partner], ffn_in.at[partner], load_sem.at[2]),
         fetched(down_hbm, down_weight, load_sem.at[3]),
-        fetched(ffn_hbm.at[partner], ffn_in.at[partner], load_sem.at[4]),
-        fetched(cot_hbm.at[partner], cot.at[partner], load_sem.at[5]),
+        fetched(cot_hbm, cot, load_sem.at[4]),
+        fetched(middle_hbm, middle, load_sem.at[5]),
     ]
 
     def units(rows):
         def one(n, carry):
             columns = pl.ds(pl.multiple_of(n * 512, 512), 512)
             value = dot(ffn_in[rows], up_weight[:, columns])
-            grad = dot(cot[rows], down_weight[:, columns])
             square = value * value
             bend = jnp.tanh(SLOPE * value * (1.0 + CUBIC * square))
             half = 0.5 * (1.0 + bend)
             hidden[rows, columns] = (value * half).astype(bf16)
             slope = half + 0.5 * value * (1.0 - bend * bend) * SLOPE * (1.0 + 3.0 * CUBIC * square)
-            grad_up[rows, columns] = (grad * slope).astype(bf16)
+            grad_up[rows, columns] = slope.astype(bf16)
+            return carry
+
+        lax.fori_loop(0, PART // 512, one, 0)
+
+    def units_back(rows):
+        def one(n, carry):
+            columns = pl.ds(pl.multiple_of(n * 512, 512), 512)
+            grad = dot(cot[rows], down_weight[:, columns])
+            grad_up[rows, columns] = (grad * grad_up[rows, columns].astype(f32)).astype(bf16)
             return carry
 
         lax.fori_loop(0, PART // 512, one, 0)
@@ -1143,7 +1186,7 @@
 
         lax.fori_loop(0, WIDTH // 512, one, 0)
 
-    def weight_grad(left, right, target):
+    def weight_grad(left, right, target, first=0, last=WIDTH // 256):
         def one(n, carry):
             columns = pl.ds(pl.multiple_of(n * 256, 256), 256)
             value = outer_dot(left[:, columns], right[...]).astype(bf16)
@@ -1151,34 +1194,54 @@
                 target[lax.div(n, 4), lax.rem(n, 4), j] = value[64 * j : 64 * j + 64]
             return carry
 
-        lax.fori_loop(0, WIDTH // 256, one, 0)
-
-    near, rest = pl.ds(0, 512), pl.ds(512, 512)
-    for load in loads[:4]:
-        load.wait()
+        lax.fori_loop(first, last, one, 0)
+
+    loads[0].wait()
+    loads[1].wait()
     units(own)
+    loads[2].wait()
+    units(partner)
+    loads[3].wait()
+    spread_out(ylo, own, hidden, down_weight, ahead)
+    ready()
+    step(ahead_sum)
+    spread_out(1 - ylo, partner, hidden, down_weight, ahead)
+    step(ahead_sum, ahead_sum)
+    loads[4].wait()
+    weight_grad(cot, hidden, grad_down_weight)
+    step(down_sum)
+    step(ahead_sum)
+    units_back(own)
+    step(down_sum)
     spread_out(ylo, own, grad_up, up_weight, back)
     step(back_sum)
-    for load in loads[4:]:
-        load.wait()
-    units(partner)
+    step(down_sum)
+    units_back(partner)
     step(back_sum)
-    weight_grad(cot, hidden.at[:, near], grad_down_weight)
-    step(down_sum)
     spread_out(1 - ylo, partner, grad_up, up_weight, back)
     step(back_sum)
-    spread_out(ylo, own, hidden, down_weight, ahead)
+    places = {}
+    for h in range(2):
+        for c in range(2):
+            place_of = (up_weight, down_weight)[h].at[:, pl.ds(512 * c, 512)]
+            places[h, c] = (place_of, fetched(out_hbm.at[c, h], place_of, load_sem.at[6 + 2 * h + c]))
+    step(down_sum)
+    weight_grad(ffn_in, grad_up, grad_up_weight, 0, 3)
     step(back_sum)
-    step(ahead_sum)
     step(down_sum)
-    spread_out(1 - ylo, partner, hidden, down_weight, ahead)
-    step(ahead_sum, ahead_sum)
+    weight_grad(ffn_in, grad_up, grad_up_weight, 3, 6)
     step(down_sum)
-    weight_grad(cot, hidden.at[:, rest], grad_down_rest)
+    weight_grad(ffn_in, grad_up, grad_up_weight, 6, 8)
+    writes = [fetched(grad_up_weight, grad_up_out, load_sem.at[0])]
     step(down_sum)
-    step(ahead_sum)
-    weight_grad(ffn_in, grad_up, grad_up_weight)
-    step(down_sum)
+    finish(ahead_sum)
+    loads[5].wait()
+
+    def end(rows):
+        layer_out[0, rows] = (middle[rows] + ahead_share[rows]).astype(bf16)
+
+    some_rows(SHARE, 32, end)
+    step(layer_move)
     finish(back_sum)
     gain = gains[pl.ds(2, 1)]
     small[...] = jnp.zeros_like(small)
@@ -1189,37 +1252,48 @@
         normed, inverse = standardize(middle[rows])
         value, grad_gain, grad_shift = norm_back(back_share[rows], normed, inverse, gain)
         here = pl.multiple_of(ylo * 512 + core * 256 + yhi * SHARE + at, 32)
-        grad_middle[rows] = value + cot[pl.ds(here, 32)].astype(f32)
+        value += cot[pl.ds(here, 32)].astype(f32)
+        grad_middle[rows] = value
+        branch_share[rows] = value.astype(bf16)
         small[pl.ds(2, 1)] += grad_gain
         small[pl.ds(3, 1)] += grad_shift
         return carry
 
     lax.fori_loop(0, SHARE // 32, back_norm, 0)
-    step(down_sum, down_sum)
-    finish(ahead_sum)
-
-    def end(rows):
-        layer_out[0, rows] = (middle[rows] + ahead_share[rows]).astype(bf16)
-
-    some_rows(SHARE, 16, end)
-    finish(down_sum)
-
-
-def feed_forward(ffn_in, cot, up, down, middle, gains):
+    writes.append(fetched(grad_middle, grad_middle_out, load_sem.at[1]))
+    for h in range(2):
+        for c in range(2):
+            place_of, load = places[h, c]
+            load.wait()
+            grad_tokens[:, pl.ds((h * 2 + c) * 512, 512)] = dot(branch_share[...], place_of[...]).astype(bf16)
+    step(heads)
+    step(layer_move)
+    finish(down_sum, heads, layer_move)
+    for write in writes:
+        write.wait()
+
+
+def feed_forward(ffn_in, cot, up, down, middle, out_weight, gains):
     return kernel_call(
         ffn_body,
-        [share_sum(), share_sum(), weight_sum(512)],
-        XZ + ["y1", "y2", "y3", "core"],
-        [(ffn_in, ANY), (cot, ANY), (up, ANY), (down, ANY), (middle, VMEM), (gains, VMEM)],
+        [share_sum(), share_sum(), weight_sum(), tokens_to_heads(), row_gather()],
+        XZ + GROUP,
+        [(ffn_in, ANY), (cot, ANY), (up, ANY), (down, ANY), (middle, ANY), (out_weight, ANY), (gains, VMEM)],
         [
-            (shaped(bf16, 2, 64, 512), VMEM),
-            (shaped(bf16, 2, 4, 4, 64, 512), VMEM),
-            (shaped(bf16, 2, 4, 4, 64, PART), VMEM),
-            (shaped(bf16, 1, SHARE, WIDTH), VMEM),
-            (shaped(f32, SHARE, WIDTH), VMEM),
-            (shaped(f32, 8, WIDTH), VMEM),
+            (shaped(bf16, 2, 64, PART), VMEM),
+            (shaped(bf16, 2, 4, 4, 64, PART), ANY),
+            (shaped(bf16, 1, 2, 2, SHARE, WIDTH), ANY),
+            (shaped(f32, SHARE, WIDTH), ANY),
+            (shaped(f32, 4, WIDTH), VMEM),
+            (shaped(bf16, SHARE, WIDTH), VMEM),
+            (shaped(bf16, 2, 2, 2, SHARE, 256), VMEM),
         ],
         [
+            pltpu.VMEM((1, SHARE, WIDTH), bf16),
+            pltpu.VMEM((SHARE, WIDTH), f32),
+            pltpu.VMEM((2, 4, 4, 64, PART), bf16),
+            pltpu.VMEM((SHARE, WIDTH), f32),
+            pltpu.VMEM((SHARE, WIDTH), bf16),
             pltpu.VMEM((1024, WIDTH), bf16),
             pltpu.VMEM((1024, WIDTH), bf16),
             pltpu.VMEM((WIDTH, PART), bf16),
@@ -1228,45 +1302,44 @@
             pltpu.VMEM((1024, PART), bf16),
             pltpu.VMEM((2, 2, 2, SHARE, WIDTH), bf16),
             pltpu.VMEM((2, 2, 2, SHARE, WIDTH), bf16),
-            pltpu.VMEM((2, 4, 4, 64, 512), bf16),
+            pltpu.VMEM((2, 4, 4, 64, PART), bf16),
             pltpu.VMEM((SHARE, WIDTH), f32),
             pltpu.VMEM((SHARE, WIDTH), f32),
-            sems(6),
+            sems(10),
         ],
         2,
         62,
     )
 
 
-def back_body(ins, outs, scratch, makers):
+def back_body(ins, outs, scratch, makers, ready):
     (
         attn_hbm,
         weight_hbm,
-        out_hbm,
-        down_hbm,
         up_hbm,
+        projected_hbm,
+        attended_hbm,
+        mask_hbm,
+        middle_hbm,
+        inputs_hbm,
+        branch_share,
+        grad_heads,
+        small_in,
+        gains,
+    ) = ins
+    input_full, sum_up, sum_qkv, sum_out, small_out, branch_full = outs
+    (
         projected,
         attended,
         mask,
         grad_middle,
         inputs_share,
-        layer_out,
-        small_in,
-        gains,
-    ) = ins
-    layer_full, input_full, sum_down, sum_up, sum_qkv, sum_out, small_out, branch_full = outs
-    (
         attn_in,
         weight,
-        out_weight,
-        grad_down_weight,
         grad_up_weight,
         grad_qkv_weight,
         grad_out_weight,
         grad_branch,
-        branch_share,
-        grad_tokens,
-        grad_heads,
         grad_projected,
         back,
         back_share,
@@ -1274,45 +1347,30 @@
         small,
         load_sem,
     ) = scratch
-    make_down, make_up, make_qkv, make_out, make_heads, make_branch, make_back, make_layer, make_input, make_small = makers
+    make_up, make_qkv, make_out, make_branch, make_back, make_input, make_small = makers
     ylo, x, z, yhi, core = place()
-    down_sum = make_down(grad_down_weight, sum_down)
     up_sum = make_up(grad_up_weight, sum_up)
     qkv_sum = make_qkv(grad_qkv_weight, sum_qkv)
     out_sum = make_out(grad_out_weight, sum_out)
-    heads = make_heads(grad_tokens, grad_heads)
     branch = make_branch(branch_share, branch_full)
     back_sum = make_back(back, back_share)
-    layer_move = make_layer(layer_out, layer_full)
     input_move = make_input(input_share, input_full)
     small_sum = make_small(small, small_out)
     loads = [
-        fetched(out_hbm, out_weight, load_sem.at[0]),
-        fetched(down_hbm, grad_down_weight, load_sem.at[1]),
-        fetched(up_hbm, grad_up_weight, load_sem.at[2]),
-        fetched(weight_hbm, weight, load_sem.at[3]),
-        fetched(attn_hbm, attn_in, load_sem.at[4]),
+        fetched(src, dst, load_sem.at[n])
+        for n, (src, dst) in enumerate(
+            (
+                (projected_hbm, projected),
+                (mask_hbm, mask),
+                (up_hbm, grad_up_weight),
+                (weight_hbm, weight),
+                (attn_hbm, attn_in),
+                (attended_hbm, attended),
+                (inputs_hbm, inputs_share),
+                (middle_hbm, grad_middle),
+            )
+        )
     ]
-
-    def low(rows):
-        branch_share[rows] = grad_middle[rows].astype(bf16)
-
-    step(layer_move)
-    some_rows(SHARE, 32, low)
-    loads[0].wait()
-    for h in range(2):
-        for c in range(2):
-            grad_tokens[:, pl.ds((h * 2 + c) * 512, 512)] = dot(
-                branch_share[...], out_weight[c, h]
-            ).astype(bf16)
-    step(heads)
-    step(branch)
-    loads[1].wait()
-    step(down_sum)
-    loads[2].wait()
-    step(up_sum)
-    step(layer_move)
-    finish(heads)
 
     def attend(r):
         for h in range(2):
@@ -1360,30 +1418,37 @@
 
         lax.fori_loop(0, WIDTH // 256, one, 0)
 
+    loads[0].wait()
+    loads[1].wait()
     attend(ylo)
-    step(down_sum)
+    ready()
+    step(branch)
+    loads[2].wait()
+    step(up_sum)
     loads[3].wait()
     spread_out(ylo)
     step(back_sum)
-    step(down_sum)
     attend(1 - ylo)
     step(back_sum)
-    step(branch)
+    step(up_sum)
     spread_out(1 - ylo)
     step(back_sum)
     step(up_sum)
     loads[4].wait()
     weight_grad(attn_in, grad_projected[...], grad_qkv_weight)
+    step(branch)
+    step(qkv_sum)
     step(back_sum)
+    step(up_sum, up_sum)
     step(qkv_sum)
-    step(down_sum, down_sum, up_sum, down_sum, down_sum)
     finish(branch)
-    gather_load = fetched(branch_full, grad_branch, load_sem.at[5])
-    step(up_sum)
+    gather_load = fetched(branch_full, grad_branch, load_sem.at[0])
+    for load in loads[5:]:
+        load.wait()
+    step(qkv_sum, up_sum)
     gather_load.wait()
     weight_grad(grad_branch, attended[...].reshape(1024, 256), grad_out_weight)
     step(out_sum)
-    step(up_sum)
     finish(back_sum)
     gain = gains[pl.ds(0, 1)]
     small[...] = small_in[...]
@@ -1398,88 +1463,80 @@
         return carry
 
     lax.fori_loop(0, SHARE // 32, back_norm, 0)
-    step(input_move, small_sum)
-    step(qkv_sum, qkv_sum, up_sum, out_sum, out_sum)
-    step(small_sum)
-    step(up_sum, qkv_sum, qkv_sum, out_sum, out_sum)
-    step(input_move)
-    step(qkv_sum, out_sum, qkv_sum, out_sum)
-    finish(layer_move, input_move, small_sum, down_sum, up_sum, qkv_sum, out_sum)
+    step(small_sum, input_move)
+    step(up_sum, qkv_sum, out_sum, out_sum)
+    step(small_sum, qkv_sum, out_sum, qkv_sum)
+    step(small_sum, out_sum, qkv_sum, out_sum)
+    step(qkv_sum, out_sum, input_move)
+    finish(input_move, small_sum, up_sum, qkv_sum, out_sum)
 
 
 def attention_back(
     attn_in,
     weight,
-    out_weight,
-    grad_down_weight,
     grad_up_weight,
     projected,
     attended,
     mask,
     grad_middle,
     inputs_share,
-    layer_out,
+    branch_share,
+    grad_heads,
     small,
     gains,
 ):
     return kernel_call(
         back_body,
         [
-            weight_sum(512),
             weight_sum(),
             weight_sum(768),
             weight_sum(256),
-            tokens_to_heads(),
             share_gather(),
             share_sum(),
             row_gather(),
-            row_gather(),
             small_reduce(),
         ],
-        DP + MP + GROUP,
+        XZ + ["x2", "z2"] + GROUP,
         [
             (attn_in, ANY),
             (weight, ANY),
-            (out_weight, ANY),
-            (grad_down_weight, ANY),
             (grad_up_weight, ANY),
-            (projected, VMEM),
-            (attended, VMEM),
-            (mask, VMEM),
-            (grad_middle, VMEM),
-            (inputs_share, VMEM),
-            (layer_out, VMEM),
+            (projected, ANY),
+            (attended, ANY),
+            (mask, ANY),
+            (grad_middle, ANY),
+            (inputs_share, ANY),
+            (branch_share, VMEM),
+            (grad_heads, VMEM),
             (small, VMEM),
             (gains, VMEM),
         ],
         [
             (shaped(bf16, 1, 2, 2, SHARE, WIDTH), ANY),
-            (shaped(bf16, 1, 2, 2, SHARE, WIDTH), ANY),
-            (shaped(bf16, 2, 64, 512), VMEM),
             (shaped(bf16, 2, 64, PART), VMEM),
             (shaped(bf16, 2, 64, 768), VMEM),
             (shaped(bf16, 2, 64, 256), VMEM),
-            (shaped(f32, 8, 128), VMEM),
+            (shaped(f32, 4, 128), VMEM),
             (shaped(bf16, 2, 2, 2, SHARE, WIDTH), ANY),
         ],
         [
+            pltpu.VMEM((2, 512, 768), bf16),
+            pltpu.VMEM((2, 2, 2, SHARE, 256), bf16),
+            pltpu.VMEM((2, 512, 512), bf16),
+            pltpu.VMEM((SHARE, WIDTH), f32),
+            pltpu.VMEM((SHARE, WIDTH), f32),
             pltpu.VMEM((1024, WIDTH), bf16),
             pltpu.VMEM((WIDTH, 768), bf16),
-            pltpu.VMEM((2, 2, WIDTH, 512), bf16),
-            pltpu.VMEM((2, 4, 4, 64, 512), bf16),
             pltpu.VMEM((2, 4, 4, 64, PART), bf16),
             pltpu.VMEM((2, 4, 4, 64, 768), bf16),
             pltpu.VMEM((2, 4, 4, 64, 256), bf16),
             pltpu.VMEM((2, 2, 2, SHARE, WIDTH), bf16),
-            pltpu.VMEM((SHARE, WIDTH), bf16),
-            pltpu.VMEM((SHARE, WIDTH), bf16),
-            pltpu.VMEM((2, 2, 2, SHARE, 256), bf16),
             pltpu.VMEM((1024, 768), bf16),
             pltpu.VMEM((2, 2, 2, SHARE, WIDTH), bf16),
             pltpu.VMEM((SHARE, WIDTH), f32),
             pltpu.VMEM((1, SHARE, WIDTH), bf16),
-            pltpu.VMEM((8, WIDTH), f32),
-            sems(6),
+            pltpu.VMEM((4, WIDTH), f32),
+            sems(8),
         ],
         3,
         62,
@@ -1533,38 +1590,37 @@
         w_down,
         norms,
     )
-    sum_down, grad_down_rest, grad_up_weight, layer_out, grad_middle, small = feed_forward(
+    sum_down, grad_up_weight, layer_out, grad_middle, small, branch_share, grad_heads = feed_forward(
         ffn_in.reshape(1024, WIDTH),
         cot.reshape(1024, WIDTH),
         up_full.reshape(WIDTH, PART),
         down_full.reshape(WIDTH, PART),
         middle,
+        out_full.reshape(2, 2, WIDTH, 512),
         gains,
     )
-    layer_out, input_grad, sum_down_rest, sum_up, sum_qkv, sum_out, small, _ = attention_back(
+    input_grad, sum_up, sum_qkv, sum_out, small, _ = attention_back(
         attn_in.reshape(1024, WIDTH),
         qkv_full.reshape(WIDTH, 768),
-        out_full.reshape(2, 2, WIDTH, 512),
-        grad_down_rest,
         grad_up_weight,
         projected,
         attended,
         allowed,
         grad_middle,
         inputs_share,
-        layer_out,
+        branch_share,
+        grad_heads,
         small,
         gains,
     )
 
-    sum_down = jnp.concatenate([sum_down, sum_down_rest], axis=2)
     sum_qkv, sum_out, sum_up, sum_down = (g.astype(f32) for g in (sum_qkv, sum_out, sum_up, sum_down))
     out_qkv = sum_qkv.reshape(2, 64, 3, 256).transpose(1, 2, 0, 3).reshape(64, 3, 512)
     out_out = sum_out.transpose(1, 0, 2).reshape(64, 512)
     out_up = sum_up.transpose(1, 0, 2).reshape(64, WIDTH)
     out_down = sum_down.transpose(1, 0, 2).reshape(64, WIDTH)
     odd = lax.rem(z, 2) == 1
-    small = jnp.where(odd, small[:4, 64:], small[:4, :64])
+    small = jnp.where(odd, small[:, 64:], small[:, :64])
     return (
         layer_out.reshape(1, 512, WIDTH).astype(f32),
         input_grad.reshape(1, 512, WIDTH).astype(f32),

time: 304 us -> 277 us (0.911)
  Pallas kernels: 283 us -> 257 us
    pallas_call x3, Pallas kernels: 283 us -> 257 us  [kernel_call(): pl.pallas_call(kernel, out_shape=[shape for shape, _ in outs], in_specs=[...]
where the time goes in v1:
time: 277 us; the launch traced here: 273 us
  Pallas kernels  257 us (93%)
  other arithmetic  7.56 us (3%)
  local copies, waits for them, and re-layouts  7.29 us (3%)
    pallas_call x3, Pallas kernels, kernel_call(): pl.pallas_call(kernel, out_shape=[shape for shape, _ in outs], in_specs=[...  257 us
    convert_element_type x1, other arithmetic, on_device(): input_grad.reshape(1, 512, WIDTH).astype(f32)  6.74 us

profile of v1, /device:TPU:16, one launch (start us, length us, event | category | flops | bytes accessed | tf_op | source)
XLA Modules:
  0.0 273.0 jit_solution(16972990378262326238)
XLA Ops:
  0.6 1.0 reshape.105
  1.6 0.2 copy.39
  1.8 0.9 reshape.106.refs_6_
  2.7 0.8 stack.23
  3.5 0.7 pad_maximum_fusion.refs_10_
  4.1 102.2 %shard_map.213 = (bf16[1,2,2,2,128,2048]{5,4,3,2,1,0:T(8,128)(2,1)}, bf16[2,4,4,64,768]{4,3,2,1,0:T(8,128)(2,1)}, bf16[2,4,4,4,64,512]{5,4,3,2,1,0:T(8,128)(2,1)...) custom-call(s32[1,512]{1,0:T(1,128)} %refs_0_.1, ...), custom_call_target="tpu_custom_call" | custom-call | tf_op jit(solution)/shard_map/pallas_call | solution.py:125
  106.3 79.1 %shard_map.214 = (bf16[2,64,1024]{2,1,0:T(8,128)(2,1)}, bf16[2,4,4,64,1024]{4,3,2,1,0:T(8,128)(2,1)}, bf16[1,2,2,128,2048]{4,3,2,1,0:T(8,128)(2,1)}, f32[128,204...) custom-call(bf16[1024,2048]{1,0:T(8,128)(2,1)} %bitcast.50, ...), custom_call_target="tpu_custom_call" | custom-call | tf_op jit(solution)/shard_map/pallas_call | solution.py:125
  185.4 75.7 %shard_map.215 = (bf16[1,2,2,128,2048]{4,3,2,1,0:T(8,128)(2,1)}, bf16[2,64,1024]{2,1,0:T(8,128)(2,1)}, bf16[2,64,768]{2,1,0:T(8,128)(2,1)}, bf16[2,64,256]{2,1,0...) custom-call(bf16[1024,2048]{1,0:T(8,128)(2,1)} %bitcast.48, bf16[2048,768]{1,0:T(8,128)(2,1)} %bitcast.53, ...), custom_call_target="tpu_custom_call" | custom-call | tf_op jit(solution)/shard_map/pallas_call | solution.py:125
  261.1 0.0 copy-start.2
  261.1 0.0 copy-start.1
  261.1 6.7 %bitcast_convert_fusion = (f32[1,512,2048]{2,1,0:T(8,128)}, f32[1,512,2048]{2,1,0:T(8,128)}) fusion(bf16[1,2,2,128,2048]{4,3,2,1,0:T(8,128)(2,1)} %get-tuple-element.54, bf16[1,2,2,128,2048]{4,3,2,1,0:T(8,128)(2,1)} %get-tuple-element.42), kind=kLoop, calls=%fused_computation | loop fusion | flops 2097152 | bytes 12582912 | tf_op jit(solution)/shard_map/convert_element_type | solution.py:1626
  267.8 0.0 copy-start.3
  267.8 0.0 copy-start.4
  267.8 0.0 copy-start
  267.8 0.0 copy-done.2
  267.9 0.2 reshape.138
  268.1 0.3 copy.31
  268.4 1.1 reshape.126
  269.4 0.0 copy-done.1
  269.5 0.8 copy.36
  270.3 0.0 copy-done.3
  270.3 0.7 copy.35
  271.0 0.0 copy-done.4
  271.0 0.1 slice_select_fusion
  271.1 0.5 slice_bitcast_fusion
  271.6 0.0 copy-done
  271.7 0.8 copy.37
  (3 shorter events, 0.1 us)
Async XLA Ops:
  261.1 6.8 %copy-start.2 = (bf16[2,64,768]{2,1,0:T(8,128)(2,1)S(1)}, bf16[2,64,768]{2,1,0:T(8,128)(2,1)}, u32[]{:S(2)}) copy-start(bf16[2,64,768]{2,1,0:T(8,128)(2,1)} %get-tuple-element.56) | copy-start | bytes 589828
  261.1 8.4 %copy-start.1 = (bf16[2,64,1024]{2,1,0:T(8,128)(2,1)S(1)}, bf16[2,64,1024]{2,1,0:T(8,128)(2,1)}, u32[]{:S(2)}) copy-start(bf16[2,64,1024]{2,1,0:T(8,128)(2,1)} %get-tuple-element.58) | copy-start | bytes 786436
  267.8 2.5 copy-start.3
  267.8 3.2 %copy-start.4 = (f32[4,128]{1,0:T(4,128)S(1)}, f32[4,128]{1,0:T(4,128)}, u32[]{:S(2)}) copy-start(f32[4,128]{1,0:T(4,128)} %get-tuple-element.55) | copy-start | bytes 6148
  267.8 3.8 %copy-start = (bf16[2,64,1024]{2,1,0:T(8,128)(2,1)S(1)}, bf16[2,64,1024]{2,1,0:T(8,128)(2,1)}, u32[]{:S(2)}) copy-start(bf16[2,64,1024]{2,1,0:T(8,128)(2,1)} %get-tuple-element.59) | copy-start | bytes 786436

commit v2 on v1

--- a/solution.py
+++ b/solution.py
@@ -529,7 +529,7 @@
     return [[xz_neighbour(axis, d) for d in SIGNS] for axis in (0, 1)]
 
 
-def weight_gather(columns, spread=False, flat=False):
+def weight_gather(columns, spread=False, flat=False, phases=(0, 1)):
     count = 4 if spread else 2
 
     def steps(own, full, local_sem, swap_send, swap_recv, send, recv):
@@ -560,16 +560,6 @@
                 return own.at[:, pl.ds(pl.multiple_of(n * columns, columns), columns)]
             return own.at[n]
 
-        mine = own if spread else half(ylo)
-        here = full.at[origin(0), x, z]
-        local = pltpu.make_async_copy(mine, here, local_sem)
-        swaps = []
-        for s in range(1, count):
-            peer = y_peer((4 - offsets[s]) % 4) if spread else lo_partner()
-            src = own if spread else half(1 - ylo)
-            swaps.append(remote(src, here, swap_send.at[s], swap_recv.at[s], peer))
-        for swap in swaps:
-            swap.start()
         sent = []
 
         def go(*args):
@@ -577,68 +567,90 @@
             copy.start()
             sent.append(copy)
 
-        def begin(s, source):
-            for r in range(2):
-                for d in range(2):
-                    src = source.at[rows_of(r)]
-                    go(src, block(s, r, 0, 0, rows_of(r)), s, r, 0, d, r)
-            for r in range(2):
-                for d in range(2):
-                    src = source.at[rows_of(r)]
-                    go(src, block(s, r, 0, 0, rows_of(r)), s, r, 2, d, 1 - r)
-
-        begin(0, mine)
-        local.start()
-        yield
-        for s in range(1, count):
-            came = full.at[origin(s), x, z]
-            remote(came, came, swap_send.at[s], swap_recv.at[s], lo_partner()).wait_recv()
-            begin(s, came)
-        yield
-        for s in range(count):
-            for r in range(2):
-                for d in range(2):
-                    came = block(s, r, -SIGNS[d], 0, rows_of(r))
-                    move(came, came, s, r, 0, d, r).wait_recv()
-                    piece = block(s, r, -SIGNS[d], 0, rows_of(r, d))
-                    go(piece, piece, s, r, 1, d, r)
-                for part in (1, 2):
+        swaps = []
+        if 0 in phases:
+            mine = own if spread else half(ylo)
+            here = full.at[origin(0), x, z]
+            local = pltpu.make_async_copy(mine, here, local_sem)
+            for s in range(1, count):
+                peer = y_peer((4 - offsets[s]) % 4) if spread else lo_partner()
+                src = own if spread else half(1 - ylo)
+                swaps.append(remote(src, here, swap_send.at[s], swap_recv.at[s], peer))
+            for swap in swaps:
+                swap.start()
+            def begin(s, source):
+                for r in range(2):
                     for d in range(2):
-                        came = block(s, r, offsets[part], 0, rows_of(r))
-                        go(came, came, s, r, 2 + part, d, 1 - r)
-            if s % 2:
-                yield
-        for s in range(count):
-            for r in range(2):
-                for d in range(2):
-                    piece = block(s, r, 2, 0, rows_of(r, d))
-                    move(piece, piece, s, r, 1, d, r).wait_recv()
-                for d in range(2):
-                    came = block(s, r, 2, 0, rows_of(r))
-                    go(came, came, s, r, 5, d, 1 - r)
-            if s % 2:
-                yield
+                        src = source.at[rows_of(r)]
+                        go(src, block(s, r, 0, 0, rows_of(r)), s, r, 0, d, r)
+                for r in range(2):
+                    for d in range(2):
+                        src = source.at[rows_of(r)]
+                        go(src, block(s, r, 0, 0, rows_of(r)), s, r, 2, d, 1 - r)
+
+            begin(0, mine)
+            local.start()
+            yield
+            for s in range(1, count):
+                came = full.at[origin(s), x, z]
+                remote(came, came, swap_send.at[s], swap_recv.at[s], lo_partner()).wait_recv()
+                begin(s, came)
+            yield
+            for s in range(count):
+                for r in range(2):
+                    for d in range(2):
+                        came = block(s, r, -SIGNS[d], 0, rows_of(r))
+                        move(came, came, s, r, 0, d, r).wait_recv()
+                        piece = block(s, r, -SIGNS[d], 0, rows_of(r, d))
+                        go(piece, piece, s, r, 1, d, r)
+                    for part in (1, 2):
+                        for d in range(2):
+                            came = block(s, r, offsets[part], 0, rows_of(r))
+                            go(came, came, s, r, 2 + part, d, 1 - r)
+                if s % 2:
+                    yield
+            for s in range(count):
+                for r in range(2):
+                    for d in range(2):
+                        piece = block(s, r, 2, 0, rows_of(r, d))
+                        move(piece, piece, s, r, 1, d, r).wait_recv()
+                    for d in range(2):
+                        came = block(s, r, 2, 0, rows_of(r))
+                        go(came, came, s, r, 5, d, 1 - r)
+                if s % 2:
+                    yield
+
+        def line_came(part, s, r, d):
+            came = block(s, r, offsets[part], -SIGNS[d], rows_of(r))
+            if 0 in phases:
+                move(came, came, s, r, 2 + part, d, 1 - r).wait_recv()
+            return came
+
         for part in (0, 2, 1, 3):
             d = part // 2
             for s in range(count):
                 for r in range(2):
-                    came = block(s, r, offsets[part], -SIGNS[d], rows_of(r))
-                    move(came, came, s, r, 2 + part, d, 1 - r).wait_recv()
-                    go(came, came, s, r, 6 + part % 2, d, 1 - r)
-            yield
+                    came = line_came(part, s, r, d)
+                    if 1 in phases:
+                        go(came, came, s, r, 6 + part % 2, d, 1 - r)
+            if 0 in phases:
+                yield
         for s in range(count):
             for r in range(2):
                 for part in range(4):
-                    d = 1 - part // 2
-                    came = block(s, r, offsets[part], -SIGNS[d], rows_of(r))
-                    move(came, came, s, r, 2 + part, d, 1 - r).wait_recv()
-                for part in range(4):
-                    d = part // 2
-                    came = block(s, r, offsets[part], 2, rows_of(r))
-                    move(came, came, s, r, 6 + part % 2, d, 1 - r).wait_recv()
+                    line_came(part, s, r, 1 - part // 2)
+        if 0 in phases:
+            local.wait()
+        yield
+        if 1 in phases:
+            for s in range(count):
+                for r in range(2):
+                    for part in range(4):
+                        d = part // 2
+                        came = block(s, r, offsets[part], 2, rows_of(r))
+                        move(came, came, s, r, 6 + part % 2, d, 1 - r).wait_recv()
         for copy in sent + swaps:
             copy.wait_send()
-        local.wait()
 
     return {
         "scratch": [pltpu.SemaphoreType.DMA, sems(count), sems(count), sems(32 * count), sems(32 * count)],
@@ -986,34 +998,48 @@
     step(heads)
     step(out, up)
     project(ylo)
-    finish(out)
-    swap = remote(
-        out_weight.at[core], out_weight.at[core], swap_send.at[2], swap_recv.at[2], core_partner()
-    )
-    swap.start()
+
+    def swap(n, half_core):
+        apart = (0, 1, -1, 2)[n // 2]
+        if n % 2 == 0:
+            here = out_weight.at[half_core, :, :, ring(z, apart), pl.ds(0, 32)]
+        else:
+            here = out_weight.at[half_core, :, ring(x, apart), :, pl.ds(32, 32)]
+        return remote(here, here, swap_send.at[2 + n], swap_recv.at[2 + n], core_partner())
+
+    step(out)
+    for n in range(6):
+        swap(n, core).start()
     step(down)
     attend(ylo)
     step(heads)
+    finish(out)
+    for n in (6, 7):
+        swap(n, core).start()
     step(up, down)
     finish(heads)
-    there = out_weight.at[1 - core]
-    remote(there, there, swap_send.at[2], swap_recv.at[2], core_partner()).wait_recv()
-    writes.append(fetched(out_weight, out_weight_out, load_sem.at[4]))
     writes.append(fetched(projected, projected_out, load_sem.at[5]))
     writes.append(fetched(attended, attended_out, load_sem.at[6]))
 
-    def branch(n, carry):
-        columns = pl.ds(pl.multiple_of(n * 256, 256), 256)
-        value = inputs_share[:, columns]
-        for c in range(2):
+    def branch(c, before):
+        def one(n, carry):
+            columns = pl.ds(pl.multiple_of(n * 512, 512), 512)
+            value = before[:, columns]
             for h in range(2):
-                features = pl.ds((h * 2 + c) * 512, 512)
-                part = out_weight[c, h * 2 + lax.div(n, 4), lax.rem(n, 4)].reshape(256, 512)
+                features = pl.ds(pl.multiple_of((h * 2 + c) * 512, 512), 512)
+                pair = pl.ds(lax.rem(n, 2) * 2, 2)
+                part = out_weight[c, h * 2 + lax.div(n, 2), pair].reshape(512, 512)
                 value += turned_dot(tokens[:, features], part)
-        middle[:, columns] = value
-        return carry
-
-    lax.fori_loop(0, WIDTH // 256, branch, 0)
+            middle[:, columns] = value
+            return carry
+
+        lax.fori_loop(0, WIDTH // 512, one, 0)
+
+    branch(core, inputs_share)
+    for n in range(8):
+        swap(n, 1 - core).wait_recv()
+    writes.append(fetched(out_weight, out_weight_out, load_sem.at[4]))
+    branch(1 - core, middle)
     gain_two, shift_two = gains[pl.ds(2, 1)], gains[pl.ds(3, 1)]
 
     def norm_two(rows):
@@ -1033,7 +1059,8 @@
     finish(spread, up, down)
     for write in writes:
         write.wait()
-    swap.wait_send()
+    for n in range(8):
+        swap(n, core).wait_send()
 
 
 def forward(ids, segments, padding, stream, cot, codebook, own_qkv, own_out, own_up, own_down, norms):
@@ -1101,8 +1128,8 @@
             pltpu.VMEM((SHARE, WIDTH), bf16),
             pltpu.VMEM((SHARE, WIDTH), bf16),
             sems(8),
-            sems(3),
-            sems(3),
+            sems(10),
+            sems(10),
         ],
         0,
     )

time: 277 us -> 272 us (0.982)
  Pallas kernels: 257 us -> 252 us
    pallas_call x3, Pallas kernels: 257 us -> 252 us  [kernel_call(): pl.pallas_call(kernel, out_shape=[shape for shape, _ in outs], in_specs=[...]
where the time goes in v2:
time: 272 us; the launch traced here: 268 us
  Pallas kernels  252 us (93%)
  other arithmetic  7.56 us (3%)
  local copies, waits for them, and re-layouts  7.29 us (3%)
    pallas_call x3, Pallas kernels, kernel_call(): pl.pallas_call(kernel, out_shape=[shape for shape, _ in outs], in_specs=[...  252 us
    convert_element_type x1, other arithmetic, on_device(): input_grad.reshape(1, 512, WIDTH).astype(f32)  6.74 us

profile of v2, /device:TPU:16, one launch (start us, length us, event | category | flops | bytes accessed | tf_op | source)
XLA Modules:
  0.0 267.6 jit_solution(14526726634422176814)
XLA Ops:
  0.6 1.0 reshape.105
  1.6 0.2 copy.39
  1.8 0.9 reshape.106.refs_6_
  2.7 0.8 stack.23
  3.5 0.7 pad_maximum_fusion.refs_10_
  4.1 97.9 %shard_map.213 = (bf16[1,2,2,2,128,2048]{5,4,3,2,1,0:T(8,128)(2,1)}, bf16[2,4,4,64,768]{4,3,2,1,0:T(8,128)(2,1)}, bf16[2,4,4,4,64,512]{5,4,3,2,1,0:T(8,128)(2,1)...) custom-call(s32[1,512]{1,0:T(1,128)} %refs_0_.1, ...), custom_call_target="tpu_custom_call" | custom-call | tf_op jit(solution)/shard_map/pallas_call | solution.py:125
  102.1 77.9 %shard_map.214 = (bf16[2,64,1024]{2,1,0:T(8,128)(2,1)}, bf16[2,4,4,64,1024]{4,3,2,1,0:T(8,128)(2,1)}, bf16[1,2,2,128,2048]{4,3,2,1,0:T(8,128)(2,1)}, f32[128,204...) custom-call(bf16[1024,2048]{1,0:T(8,128)(2,1)} %bitcast.50, ...), custom_call_target="tpu_custom_call" | custom-call | tf_op jit(solution)/shard_map/pallas_call | solution.py:125
  179.9 75.8 %shard_map.215 = (bf16[1,2,2,128,2048]{4,3,2,1,0:T(8,128)(2,1)}, bf16[2,64,1024]{2,1,0:T(8,128)(2,1)}, bf16[2,64,768]{2,1,0:T(8,128)(2,1)}, bf16[2,64,256]{2,1,0...) custom-call(bf16[1024,2048]{1,0:T(8,128)(2,1)} %bitcast.48, bf16[2048,768]{1,0:T(8,128)(2,1)} %bitcast.53, ...), custom_call_target="tpu_custom_call" | custom-call | tf_op jit(solution)/shard_map/pallas_call | solution.py:125
  255.7 0.0 copy-start.2
  255.7 0.0 copy-start.1
  255.7 6.7 %bitcast_convert_fusion = (f32[1,512,2048]{2,1,0:T(8,128)}, f32[1,512,2048]{2,1,0:T(8,128)}) fusion(bf16[1,2,2,128,2048]{4,3,2,1,0:T(8,128)(2,1)} %get-tuple-element.54, bf16[1,2,2,128,2048]{4,3,2,1,0:T(8,128)(2,1)} %get-tuple-element.42), kind=kLoop, calls=%fused_computation | loop fusion | flops 2097152 | bytes 12582912 | tf_op jit(solution)/shard_map/convert_element_type | solution.py:1653
  262.5 0.0 copy-start.3
  262.5 0.0 copy-start.4
  262.5 0.0 copy-start
  262.5 0.0 copy-done.2
  262.5 0.2 reshape.138
  262.7 0.3 copy.31
  263.0 1.1 reshape.126
  264.1 0.0 copy-done.1
  264.1 0.8 copy.36
  265.0 0.0 copy-done.3
  265.0 0.7 copy.35
  265.6 0.0 copy-done.4
  265.6 0.1 slice_select_fusion
  265.7 0.5 slice_bitcast_fusion
  266.2 0.0 copy-done
  266.3 0.8 copy.37
  (3 shorter events, 0.1 us)
Async XLA Ops:
  255.7 6.8 %copy-start.2 = (bf16[2,64,768]{2,1,0:T(8,128)(2,1)S(1)}, bf16[2,64,768]{2,1,0:T(8,128)(2,1)}, u32[]{:S(2)}) copy-start(bf16[2,64,768]{2,1,0:T(8,128)(2,1)} %get-tuple-element.56) | copy-start | bytes 589828
  255.7 8.4 %copy-start.1 = (bf16[2,64,1024]{2,1,0:T(8,128)(2,1)S(1)}, bf16[2,64,1024]{2,1,0:T(8,128)(2,1)}, u32[]{:S(2)}) copy-start(bf16[2,64,1024]{2,1,0:T(8,128)(2,1)} %get-tuple-element.58) | copy-start | bytes 786436
  262.5 2.5 copy-start.3
  262.5 3.2 %copy-start.4 = (f32[4,128]{1,0:T(4,128)S(1)}, f32[4,128]{1,0:T(4,128)}, u32[]{:S(2)}) copy-start(f32[4,128]{1,0:T(4,128)} %get-tuple-element.55) | copy-start | bytes 6148
  262.5 3.8 %copy-start = (bf16[2,64,1024]{2,1,0:T(8,128)(2,1)S(1)}, bf16[2,64,1024]{2,1,0:T(8,128)(2,1)}, u32[]{:S(2)}) copy-start(bf16[2,64,1024]{2,1,0:T(8,128)(2,1)} %get-tuple-element.59) | copy-start | bytes 786436

commit v3 on v2

--- a/solution.py
+++ b/solution.py
@@ -1491,10 +1491,9 @@
 
     lax.fori_loop(0, SHARE // 32, back_norm, 0)
     step(small_sum, input_move)
-    step(up_sum, qkv_sum, out_sum, out_sum)
-    step(small_sum, qkv_sum, out_sum, qkv_sum)
-    step(small_sum, out_sum, qkv_sum, out_sum)
-    step(qkv_sum, out_sum, input_move)
+    step(up_sum, out_sum, qkv_sum, small_sum, out_sum, qkv_sum, out_sum, small_sum, qkv_sum)
+    step(out_sum, qkv_sum, out_sum)
+    step(out_sum, qkv_sum, input_move)
     finish(input_move, small_sum, up_sum, qkv_sum, out_sum)
 
 

time: 272 us -> 273 us (level)
  no operation moved by 1% of the time
where the time goes in v3:
time: 273 us; the launch traced here: 268 us
  Pallas kernels  252 us (92%)
  other arithmetic  7.56 us (3%)
  local copies, waits for them, and re-layouts  7.29 us (3%)
    pallas_call x3, Pallas kernels, kernel_call(): pl.pallas_call(kernel, out_shape=[shape for shape, _ in outs], in_specs=[...  252 us
    convert_element_type x1, other arithmetic, on_device(): input_grad.reshape(1, 512, WIDTH).astype(f32)  6.74 us

profile of v3, /device:TPU:16, one launch (start us, length us, event | category | flops | bytes accessed | tf_op | source)
XLA Modules:
  0.0 268.3 jit_solution(8392008717148013462)
XLA Ops:
  0.6 1.0 reshape.105
  1.6 0.2 copy.39
  1.8 0.9 reshape.106.refs_6_
  2.7 0.8 stack.23
  3.5 0.7 pad_maximum_fusion.refs_10_
  4.1 97.9 %shard_map.213 = (bf16[1,2,2,2,128,2048]{5,4,3,2,1,0:T(8,128)(2,1)}, bf16[2,4,4,64,768]{4,3,2,1,0:T(8,128)(2,1)}, bf16[2,4,4,4,64,512]{5,4,3,2,1,0:T(8,128)(2,1)...) custom-call(s32[1,512]{1,0:T(1,128)} %refs_0_.1, ...), custom_call_target="tpu_custom_call" | custom-call | tf_op jit(solution)/shard_map/pallas_call | solution.py:125
  102.1 77.9 %shard_map.214 = (bf16[2,64,1024]{2,1,0:T(8,128)(2,1)}, bf16[2,4,4,64,1024]{4,3,2,1,0:T(8,128)(2,1)}, bf16[1,2,2,128,2048]{4,3,2,1,0:T(8,128)(2,1)}, f32[128,204...) custom-call(bf16[1024,2048]{1,0:T(8,128)(2,1)} %bitcast.50, ...), custom_call_target="tpu_custom_call" | custom-call | tf_op jit(solution)/shard_map/pallas_call | solution.py:125
  179.9 76.5 %shard_map.215 = (bf16[1,2,2,128,2048]{4,3,2,1,0:T(8,128)(2,1)}, bf16[2,64,1024]{2,1,0:T(8,128)(2,1)}, bf16[2,64,768]{2,1,0:T(8,128)(2,1)}, bf16[2,64,256]{2,1,0...) custom-call(bf16[1024,2048]{1,0:T(8,128)(2,1)} %bitcast.48, bf16[2048,768]{1,0:T(8,128)(2,1)} %bitcast.53, ...), custom_call_target="tpu_custom_call" | custom-call | tf_op jit(solution)/shard_map/pallas_call | solution.py:125
  256.4 0.0 copy-start.2
  256.4 0.0 copy-start.1
  256.4 6.7 %bitcast_convert_fusion = (f32[1,512,2048]{2,1,0:T(8,128)}, f32[1,512,2048]{2,1,0:T(8,128)}) fusion(bf16[1,2,2,128,2048]{4,3,2,1,0:T(8,128)(2,1)} %get-tuple-element.54, bf16[1,2,2,128,2048]{4,3,2,1,0:T(8,128)(2,1)} %get-tuple-element.42), kind=kLoop, calls=%fused_computation | loop fusion | flops 2097152 | bytes 12582912 | tf_op jit(solution)/shard_map/convert_element_type | solution.py:1652
  263.2 0.0 copy-start.3
  263.2 0.0 copy-start.4
  263.2 0.0 copy-start
  263.2 0.0 copy-done.2
  263.2 0.2 reshape.138
  263.4 0.3 copy.31
  263.7 1.1 reshape.126
  264.8 0.0 copy-done.1
  264.8 0.8 copy.36
  265.7 0.0 copy-done.3
  265.7 0.7 copy.35
  266.4 0.0 copy-done.4
  266.4 0.1 slice_select_fusion
  266.4 0.5 slice_bitcast_fusion
  267.0 0.0 copy-done
  267.0 0.8 copy.37
  (3 shorter events, 0.1 us)
Async XLA Ops:
  256.4 6.8 %copy-start.2 = (bf16[2,64,768]{2,1,0:T(8,128)(2,1)S(1)}, bf16[2,64,768]{2,1,0:T(8,128)(2,1)}, u32[]{:S(2)}) copy-start(bf16[2,64,768]{2,1,0:T(8,128)(2,1)} %get-tuple-element.56) | copy-start | bytes 589828
  256.4 8.4 %copy-start.1 = (bf16[2,64,1024]{2,1,0:T(8,128)(2,1)S(1)}, bf16[2,64,1024]{2,1,0:T(8,128)(2,1)}, u32[]{:S(2)}) copy-start(bf16[2,64,1024]{2,1,0:T(8,128)(2,1)} %get-tuple-element.58) | copy-start | bytes 786436
  263.2 2.5 copy-start.3
  263.2 3.2 %copy-start.4 = (f32[4,128]{1,0:T(4,128)S(1)}, f32[4,128]{1,0:T(4,128)}, u32[]{:S(2)}) copy-start(f32[4,128]{1,0:T(4,128)} %get-tuple-element.55) | copy-start | bytes 6148
  263.2 3.8 %copy-start = (bf16[2,64,1024]{2,1,0:T(8,128)(2,1)S(1)}, bf16[2,64,1024]{2,1,0:T(8,128)(2,1)}, u32[]{:S(2)}) copy-start(bf16[2,64,1024]{2,1,0:T(8,128)(2,1)} %get-tuple-element.59) | copy-start | bytes 786436
